TPU v7x, 256 devices: a whole 4x4x8 slice. The times are simulated.
256 devices in a mesh: seq: 32 (over z, x_hi, core), head: 8 (over x_lo, y).
Axes of the slice: x: 4 (x_hi: 2, x_lo: 2; x = x_hi * 2 + x_lo), y: 4, z: 8, core: 2. Of those that a mesh axis runs over, the one named last changes fastest.
Arguments:
- q_nope: bfloat16 [4096, 8192], P('seq', 'head'), may hold values from -6 to 6
- q_rope: bfloat16 [4096, 4096], P('seq', 'head'), may hold values from -16 to 16
- kv_latent: bfloat16 [4096, 576], P('seq'), may hold values from -500 to 500
- positions: int32 [4096], P('seq'), may hold values from 0 to 4095, as said below
- kv_gain: float32 [512], replicated, may hold values from 0.5 to 2
- kv_up: bfloat16 [512, 16384], P(None, 'head'), may hold values from -0.25 to 0.25
- w_out: bfloat16 [8192, 7168], P('head', 'seq'), may hold values from -0.125 to 0.125
Outputs:
- mixed: bfloat16 [4096, 7168], P('seq', 'head')
Inputs may be any that keep to these rules, and one draw needn't show every extreme that they name: The positions of each aligned block of 128 rows are consecutive and ascending and start at a multiple of 128; all positions together hold every number from 0 to 4095 once.
All inputs are finite; a program needn't handle non-finite values.
Results may differ from a plain program's by a relative error of at most 0.02.
Values may be sent and summed in bfloat16 or wider, within the bound.
A program may use at most 64 MiB of HBM per device.

v0:
```python
import math

import jax
import jax.numpy as jnp
from jax import lax
from jax.sharding import PartitionSpec as P

KV_RANK = 512
ROPE = 64
NOPE = 128
VDIM = 128


def shifted(block, axis, distance):
    devices = range(lax.axis_size(axis))
    route = [((i - distance) % len(devices), i) for i in devices]
    return lax.ppermute(block, axis, route)


def local(q_nope, q_rope, kv_latent, positions, kv_gain, kv_up, w_out):
    rows = q_nope.shape[0]
    heads = q_nope.shape[1] // NOPE
    count = lax.axis_size("seq")
    myself = lax.axis_index("seq")
    scale = 1.0 / math.sqrt(NOPE + ROPE)
    all_positions = lax.all_gather(positions, "seq", axis=0, tiled=True)
    coded = kv_latent[:, :KV_RANK].astype(jnp.float32)
    latent = (
        coded * lax.rsqrt(jnp.mean(coded * coded, axis=1, keepdims=True) + 1e-06) * kv_gain
    ).astype(jnp.bfloat16)
    own_block = jnp.concatenate([latent, kv_latent[:, KV_RANK:]], axis=1)
    query_nope = q_nope.reshape(rows, heads, NOPE)
    query_rope = q_rope.reshape(rows, heads, ROPE)

    def update(state, block, key_pos):
        running, total, summed = state
        width = block.shape[0]
        keys_values = jnp.dot(block[:, :KV_RANK], kv_up, preferred_element_type=jnp.float32).astype(
            jnp.bfloat16
        )
        keys_values = keys_values.reshape(width, heads, NOPE + VDIM)
        scores = jnp.einsum(
            "ihd,jhd->hij", query_nope, keys_values[:, :, :NOPE], preferred_element_type=jnp.float32
        )
        scores = scores + jnp.einsum(
            "ihd,jd->hij", query_rope, block[:, KV_RANK:], preferred_element_type=jnp.float32
        )
        visible = positions[:, None] >= key_pos[None, :]
        scores = jnp.where(visible[None], scores * scale, -1e30)
        newest = jnp.maximum(running, jnp.max(scores, axis=2))
        factor = jnp.exp(running - newest)
        expo = jnp.exp(scores - newest[:, :, None])
        total = total * factor + jnp.sum(expo, axis=2)
        summed = summed * factor[:, :, None] + jnp.einsum(
            "hij,jhd->hid",
            expo.astype(jnp.bfloat16),
            keys_values[:, :, NOPE:],
            preferred_element_type=jnp.float32,
        )
        return (newest, total, summed)

    def attend(state, block, anchor):
        width = block.shape[0]
        key_pos = lax.dynamic_slice_in_dim(all_positions, anchor * width, width)
        return update(state, block, key_pos)

    state = (
        jnp.full((heads, rows), -1e30, jnp.float32),
        jnp.zeros((heads, rows), jnp.float32),
        jnp.zeros((heads, rows, VDIM), jnp.float32),
    )
    state = attend(state, own_block, myself)

    def forward(step, carry):
        held, block = carry
        block = shifted(block, "seq", 1)
        held = attend(held, block, (myself - step) % count)
        return (held, block)

    state, unused = lax.fori_loop(1, count, forward, (state, own_block))
    running, total, summed = state
    attended = (summed / total[:, :, None]).astype(jnp.bfloat16)
    attended = attended.transpose(1, 0, 2).reshape(rows, heads * VDIM)
    partial_out = jnp.dot(
        attended,
        lax.all_gather(w_out, "seq", axis=1, tiled=True),
        preferred_element_type=jnp.float32,
    )
    return lax.psum_scatter(
        partial_out.astype(jnp.bfloat16), "head", scatter_dimension=1, tiled=True
    )


def solution(mesh):
    return jax.shard_map(
        local,
        mesh=mesh,
        in_specs=(
            P("seq", "head"),
            P("seq", "head"),
            P("seq", None),
            P("seq"),
            P(),
            P(None, "head"),
            P("head", "seq"),
        ),
        out_specs=P("seq", "head"),
        check_vma=False,
    )
```

profile of v0, /device:TPU:2, one launch (start us, length us, event | category | flops | bytes accessed | tf_op | source)
XLA Modules:
  0.0 470.9 jit_solution(244321789315426878)
XLA Ops:
  9.6 43.7 %all-gather = s32[32,1,128]{2,1,0:T(1,128)S(1)} all-gather(s32[1,1,128]{2,1,0:T(1,128)} %bitcast.77), channel_id=1, replica_groups=mesh['seq'=32,'head'=8] {'seq'}, dimensions={0}, use_global_device_ids=true | all-gather | bytes 16896 | tf_op jit(solution)/shard_map/all_gather | solution.py:26
  63.8 344.5 %while.21 = (s32[]{:T(128)}, f32[8,128]{1,0:T(8,128)S(1)}, f32[8,128]{1,0:T(8,128)S(1)}, f32[8,128,128]{2,1,0:T(8,128)S(1)}, bf16[128,576]{0,1:T(8,128)(2,1)}, /...) while((s32[]{:T(128)}, f32[8,128]{1,0:T(8,128)S(1)}, ...), condition=%wide.region_6.7_spmd, body=%wide.region_3.6_spmd.sunk | while | flops 353912832 | bytes 10439024 | solution.py:80
  65.7 8.4 %collective-permute-done = bf16[128,576]{0,1:T(8,128)(2,1)S(1)} collective-permute-done((bf16[128,576]{0,1:T(8,128)(2,1)}, bf16[128,576]{0,1:T(8,128)(2,1)S(1)}, u32[]{:S(2)}, u32[]{:S(2)}) %collective-permute-start) | collective-permute-done | bytes 147488 | tf_op jit(solution)/shard_map/while/body/eval_jaxpr/ppermute | solution.py:17
  78.0 7.0 %collective-permute-done = bf16[128,576]{0,1:T(8,128)(2,1)S(1)} collective-permute-done((bf16[128,576]{0,1:T(8,128)(2,1)}, bf16[128,576]{0,1:T(8,128)(2,1)S(1)}, u32[]{:S(2)}, u32[]{:S(2)}) %collective-permute-start) | collective-permute-done | bytes 147488 | tf_op jit(solution)/shard_map/while/body/eval_jaxpr/ppermute | solution.py:17
  89.0 7.0 %collective-permute-done = bf16[128,576]{0,1:T(8,128)(2,1)S(1)} collective-permute-done((bf16[128,576]{0,1:T(8,128)(2,1)}, bf16[128,576]{0,1:T(8,128)(2,1)S(1)}, u32[]{:S(2)}, u32[]{:S(2)}) %collective-permute-start) | collective-permute-done | bytes 147488 | tf_op jit(solution)/shard_map/while/body/eval_jaxpr/ppermute | solution.py:17
  99.9 7.0 %collective-permute-done = bf16[128,576]{0,1:T(8,128)(2,1)S(1)} collective-permute-done((bf16[128,576]{0,1:T(8,128)(2,1)}, bf16[128,576]{0,1:T(8,128)(2,1)S(1)}, u32[]{:S(2)}, u32[]{:S(2)}) %collective-permute-start) | collective-permute-done | bytes 147488 | tf_op jit(solution)/shard_map/while/body/eval_jaxpr/ppermute | solution.py:17
  110.9 6.9 %collective-permute-done = bf16[128,576]{0,1:T(8,128)(2,1)S(1)} collective-permute-done((bf16[128,576]{0,1:T(8,128)(2,1)}, bf16[128,576]{0,1:T(8,128)(2,1)S(1)}, u32[]{:S(2)}, u32[]{:S(2)}) %collective-permute-start) | collective-permute-done | bytes 147488 | tf_op jit(solution)/shard_map/while/body/eval_jaxpr/ppermute | solution.py:17
  121.7 10.0 %collective-permute-done = bf16[128,576]{0,1:T(8,128)(2,1)S(1)} collective-permute-done((bf16[128,576]{0,1:T(8,128)(2,1)}, bf16[128,576]{0,1:T(8,128)(2,1)S(1)}, u32[]{:S(2)}, u32[]{:S(2)}) %collective-permute-start) | collective-permute-done | bytes 147488 | tf_op jit(solution)/shard_map/while/body/eval_jaxpr/ppermute | solution.py:17
  135.7 10.0 %collective-permute-done = bf16[128,576]{0,1:T(8,128)(2,1)S(1)} collective-permute-done((bf16[128,576]{0,1:T(8,128)(2,1)}, bf16[128,576]{0,1:T(8,128)(2,1)S(1)}, u32[]{:S(2)}, u32[]{:S(2)}) %collective-permute-start) | collective-permute-done | bytes 147488 | tf_op jit(solution)/shard_map/while/body/eval_jaxpr/ppermute | solution.py:17
  149.6 6.9 %collective-permute-done = bf16[128,576]{0,1:T(8,128)(2,1)S(1)} collective-permute-done((bf16[128,576]{0,1:T(8,128)(2,1)}, bf16[128,576]{0,1:T(8,128)(2,1)S(1)}, u32[]{:S(2)}, u32[]{:S(2)}) %collective-permute-start) | collective-permute-done | bytes 147488 | tf_op jit(solution)/shard_map/while/body/eval_jaxpr/ppermute | solution.py:17
  160.5 6.9 %collective-permute-done = bf16[128,576]{0,1:T(8,128)(2,1)S(1)} collective-permute-done((bf16[128,576]{0,1:T(8,128)(2,1)}, bf16[128,576]{0,1:T(8,128)(2,1)S(1)}, u32[]{:S(2)}, u32[]{:S(2)}) %collective-permute-start) | collective-permute-done | bytes 147488 | tf_op jit(solution)/shard_map/while/body/eval_jaxpr/ppermute | solution.py:17
  171.3 6.9 %collective-permute-done = bf16[128,576]{0,1:T(8,128)(2,1)S(1)} collective-permute-done((bf16[128,576]{0,1:T(8,128)(2,1)}, bf16[128,576]{0,1:T(8,128)(2,1)S(1)}, u32[]{:S(2)}, u32[]{:S(2)}) %collective-permute-start) | collective-permute-done | bytes 147488 | tf_op jit(solution)/shard_map/while/body/eval_jaxpr/ppermute | solution.py:17
  182.1 6.9 %collective-permute-done = bf16[128,576]{0,1:T(8,128)(2,1)S(1)} collective-permute-done((bf16[128,576]{0,1:T(8,128)(2,1)}, bf16[128,576]{0,1:T(8,128)(2,1)S(1)}, u32[]{:S(2)}, u32[]{:S(2)}) %collective-permute-start) | collective-permute-done | bytes 147488 | tf_op jit(solution)/shard_map/while/body/eval_jaxpr/ppermute | solution.py:17
  193.0 6.9 %collective-permute-done = bf16[128,576]{0,1:T(8,128)(2,1)S(1)} collective-permute-done((bf16[128,576]{0,1:T(8,128)(2,1)}, bf16[128,576]{0,1:T(8,128)(2,1)S(1)}, u32[]{:S(2)}, u32[]{:S(2)}) %collective-permute-start) | collective-permute-done | bytes 147488 | tf_op jit(solution)/shard_map/while/body/eval_jaxpr/ppermute | solution.py:17
  225.5 6.9 %collective-permute-done = bf16[128,576]{0,1:T(8,128)(2,1)S(1)} collective-permute-done((bf16[128,576]{0,1:T(8,128)(2,1)}, bf16[128,576]{0,1:T(8,128)(2,1)S(1)}, u32[]{:S(2)}, u32[]{:S(2)}) %collective-permute-start) | collective-permute-done | bytes 147488 | tf_op jit(solution)/shard_map/while/body/eval_jaxpr/ppermute | solution.py:17
  247.2 6.9 %collective-permute-done = bf16[128,576]{0,1:T(8,128)(2,1)S(1)} collective-permute-done((bf16[128,576]{0,1:T(8,128)(2,1)}, bf16[128,576]{0,1:T(8,128)(2,1)S(1)}, u32[]{:S(2)}, u32[]{:S(2)}) %collective-permute-start) | collective-permute-done | bytes 147488 | tf_op jit(solution)/shard_map/while/body/eval_jaxpr/ppermute | solution.py:17
  258.0 6.9 %collective-permute-done = bf16[128,576]{0,1:T(8,128)(2,1)S(1)} collective-permute-done((bf16[128,576]{0,1:T(8,128)(2,1)}, bf16[128,576]{0,1:T(8,128)(2,1)S(1)}, u32[]{:S(2)}, u32[]{:S(2)}) %collective-permute-start) | collective-permute-done | bytes 147488 | tf_op jit(solution)/shard_map/while/body/eval_jaxpr/ppermute | solution.py:17
  268.8 6.9 %collective-permute-done = bf16[128,576]{0,1:T(8,128)(2,1)S(1)} collective-permute-done((bf16[128,576]{0,1:T(8,128)(2,1)}, bf16[128,576]{0,1:T(8,128)(2,1)S(1)}, u32[]{:S(2)}, u32[]{:S(2)}) %collective-permute-start) | collective-permute-done | bytes 147488 | tf_op jit(solution)/shard_map/while/body/eval_jaxpr/ppermute | solution.py:17
  279.7 6.9 %collective-permute-done = bf16[128,576]{0,1:T(8,128)(2,1)S(1)} collective-permute-done((bf16[128,576]{0,1:T(8,128)(2,1)}, bf16[128,576]{0,1:T(8,128)(2,1)S(1)}, u32[]{:S(2)}, u32[]{:S(2)}) %collective-permute-start) | collective-permute-done | bytes 147488 | tf_op jit(solution)/shard_map/while/body/eval_jaxpr/ppermute | solution.py:17
  290.5 6.9 %collective-permute-done = bf16[128,576]{0,1:T(8,128)(2,1)S(1)} collective-permute-done((bf16[128,576]{0,1:T(8,128)(2,1)}, bf16[128,576]{0,1:T(8,128)(2,1)S(1)}, u32[]{:S(2)}, u32[]{:S(2)}) %collective-permute-start) | collective-permute-done | bytes 147488 | tf_op jit(solution)/shard_map/while/body/eval_jaxpr/ppermute | solution.py:17
  301.4 6.9 %collective-permute-done = bf16[128,576]{0,1:T(8,128)(2,1)S(1)} collective-permute-done((bf16[128,576]{0,1:T(8,128)(2,1)}, bf16[128,576]{0,1:T(8,128)(2,1)S(1)}, u32[]{:S(2)}, u32[]{:S(2)}) %collective-permute-start) | collective-permute-done | bytes 147488 | tf_op jit(solution)/shard_map/while/body/eval_jaxpr/ppermute | solution.py:17
  312.2 6.9 %collective-permute-done = bf16[128,576]{0,1:T(8,128)(2,1)S(1)} collective-permute-done((bf16[128,576]{0,1:T(8,128)(2,1)}, bf16[128,576]{0,1:T(8,128)(2,1)S(1)}, u32[]{:S(2)}, u32[]{:S(2)}) %collective-permute-start) | collective-permute-done | bytes 147488 | tf_op jit(solution)/shard_map/while/body/eval_jaxpr/ppermute | solution.py:17
  323.0 6.9 %collective-permute-done = bf16[128,576]{0,1:T(8,128)(2,1)S(1)} collective-permute-done((bf16[128,576]{0,1:T(8,128)(2,1)}, bf16[128,576]{0,1:T(8,128)(2,1)S(1)}, u32[]{:S(2)}, u32[]{:S(2)}) %collective-permute-start) | collective-permute-done | bytes 147488 | tf_op jit(solution)/shard_map/while/body/eval_jaxpr/ppermute | solution.py:17
  333.9 6.9 %collective-permute-done = bf16[128,576]{0,1:T(8,128)(2,1)S(1)} collective-permute-done((bf16[128,576]{0,1:T(8,128)(2,1)}, bf16[128,576]{0,1:T(8,128)(2,1)S(1)}, u32[]{:S(2)}, u32[]{:S(2)}) %collective-permute-start) | collective-permute-done | bytes 147488 | tf_op jit(solution)/shard_map/while/body/eval_jaxpr/ppermute | solution.py:17
  344.7 6.9 %collective-permute-done = bf16[128,576]{0,1:T(8,128)(2,1)S(1)} collective-permute-done((bf16[128,576]{0,1:T(8,128)(2,1)}, bf16[128,576]{0,1:T(8,128)(2,1)S(1)}, u32[]{:S(2)}, u32[]{:S(2)}) %collective-permute-start) | collective-permute-done | bytes 147488 | tf_op jit(solution)/shard_map/while/body/eval_jaxpr/ppermute | solution.py:17
  355.5 6.9 %collective-permute-done = bf16[128,576]{0,1:T(8,128)(2,1)S(1)} collective-permute-done((bf16[128,576]{0,1:T(8,128)(2,1)}, bf16[128,576]{0,1:T(8,128)(2,1)S(1)}, u32[]{:S(2)}, u32[]{:S(2)}) %collective-permute-start) | collective-permute-done | bytes 147488 | tf_op jit(solution)/shard_map/while/body/eval_jaxpr/ppermute | solution.py:17
  366.4 6.9 %collective-permute-done = bf16[128,576]{0,1:T(8,128)(2,1)S(1)} collective-permute-done((bf16[128,576]{0,1:T(8,128)(2,1)}, bf16[128,576]{0,1:T(8,128)(2,1)S(1)}, u32[]{:S(2)}, u32[]{:S(2)}) %collective-permute-start) | collective-permute-done | bytes 147488 | tf_op jit(solution)/shard_map/while/body/eval_jaxpr/ppermute | solution.py:17
  377.2 6.9 %collective-permute-done = bf16[128,576]{0,1:T(8,128)(2,1)S(1)} collective-permute-done((bf16[128,576]{0,1:T(8,128)(2,1)}, bf16[128,576]{0,1:T(8,128)(2,1)S(1)}, u32[]{:S(2)}, u32[]{:S(2)}) %collective-permute-start) | collective-permute-done | bytes 147488 | tf_op jit(solution)/shard_map/while/body/eval_jaxpr/ppermute | solution.py:17
  388.1 6.9 %collective-permute-done = bf16[128,576]{0,1:T(8,128)(2,1)S(1)} collective-permute-done((bf16[128,576]{0,1:T(8,128)(2,1)}, bf16[128,576]{0,1:T(8,128)(2,1)S(1)}, u32[]{:S(2)}, u32[]{:S(2)}) %collective-permute-start) | collective-permute-done | bytes 147488 | tf_op jit(solution)/shard_map/while/body/eval_jaxpr/ppermute | solution.py:17
  398.9 6.9 %collective-permute-done = bf16[128,576]{0,1:T(8,128)(2,1)S(1)} collective-permute-done((bf16[128,576]{0,1:T(8,128)(2,1)}, bf16[128,576]{0,1:T(8,128)(2,1)S(1)}, u32[]{:S(2)}, u32[]{:S(2)}) %collective-permute-start) | collective-permute-done | bytes 147488 | tf_op jit(solution)/shard_map/while/body/eval_jaxpr/ppermute | solution.py:17
  408.5 10.1 %convolution_convert_fusion.1 = bf16[128,7168]{1,0:T(8,128)(2,1)S(1)} fusion(bf16[128,1024]{0,1:T(8,128)(2,1)S(1)} %bitcast.75, bf16[1024,7168]{0,1:T(8,128)(2,1)} %all-gather.3.cloned.1.call-done), kind=kOutput, calls=%fused_computation.18 | convolution fusion | flops 1879965696 | bytes 16777216 | tf_op jit(solution)/shard_map/dot_general | solution.py:84
  421.0 41.2 %reduce-scatter.4.cloned.1.call-done = bf16[896,128]{1,0:T(8,128)(2,1)} async-done(((bf16[7168,128]{1,0:T(8,128)(2,1)}), bf16[896,128]{1,0:T(8,128)(2,1)}) %reduce-scatter.4.cloned.1.call-update) | async-done | bytes 229392
  (471 shorter events, 158.5 us)
Async XLA Ops:
  6.5 402.0 %all-gather.3.cloned.1.call-start = ((), (), s32[]{:S(2)}) async-start(), calls=%async_computation.1 | async-start | bytes 15138816 | tf_op jit(solution)/shard_map/all_gather | solution.py:86
  7.3 455.0 %reduce-scatter.4.cloned.1.call-start = ((), (), s32[]{:S(2)}) async-start(), calls=%async_computation.2 | async-start | bytes 2064384
  63.8 10.3 %collective-permute-start = (bf16[128,576]{0,1:T(8,128)(2,1)}, bf16[128,576]{0,1:T(8,128)(2,1)S(1)}, u32[]{:S(2)}, u32[]{:S(2)}) collective-permute-start(bf16[128,576]{0,1:T(8,128)(2,1)} %get-tuple-element.429), channel_id=1, source_target_pairs={{248,0},{0,8},{8,16},{16,24},{24,32},{32,40},{40,48},{48,56},{56,6... | collective-permute-start | bytes 442376 | tf_op jit(solution)/shard_map/while/body/eval_jaxpr/ppermute | solution.py:17
  76.5 8.5 %collective-permute-start = (bf16[128,576]{0,1:T(8,128)(2,1)}, bf16[128,576]{0,1:T(8,128)(2,1)S(1)}, u32[]{:S(2)}, u32[]{:S(2)}) collective-permute-start(bf16[128,576]{0,1:T(8,128)(2,1)} %get-tuple-element.429), channel_id=1, source_target_pairs={{248,0},{0,8},{8,16},{16,24},{24,32},{32,40},{40,48},{48,56},{56,6... | collective-permute-start | bytes 442376 | tf_op jit(solution)/shard_map/while/body/eval_jaxpr/ppermute | solution.py:17
  87.5 8.5 %collective-permute-start = (bf16[128,576]{0,1:T(8,128)(2,1)}, bf16[128,576]{0,1:T(8,128)(2,1)S(1)}, u32[]{:S(2)}, u32[]{:S(2)}) collective-permute-start(bf16[128,576]{0,1:T(8,128)(2,1)} %get-tuple-element.429), channel_id=1, source_target_pairs={{248,0},{0,8},{8,16},{16,24},{24,32},{32,40},{40,48},{48,56},{56,6... | collective-permute-start | bytes 442376 | tf_op jit(solution)/shard_map/while/body/eval_jaxpr/ppermute | solution.py:17
  98.4 8.5 %collective-permute-start = (bf16[128,576]{0,1:T(8,128)(2,1)}, bf16[128,576]{0,1:T(8,128)(2,1)S(1)}, u32[]{:S(2)}, u32[]{:S(2)}) collective-permute-start(bf16[128,576]{0,1:T(8,128)(2,1)} %get-tuple-element.429), channel_id=1, source_target_pairs={{248,0},{0,8},{8,16},{16,24},{24,32},{32,40},{40,48},{48,56},{56,6... | collective-permute-start | bytes 442376 | tf_op jit(solution)/shard_map/while/body/eval_jaxpr/ppermute | solution.py:17
  109.4 8.4 %collective-permute-start = (bf16[128,576]{0,1:T(8,128)(2,1)}, bf16[128,576]{0,1:T(8,128)(2,1)S(1)}, u32[]{:S(2)}, u32[]{:S(2)}) collective-permute-start(bf16[128,576]{0,1:T(8,128)(2,1)} %get-tuple-element.429), channel_id=1, source_target_pairs={{248,0},{0,8},{8,16},{16,24},{24,32},{32,40},{40,48},{48,56},{56,6... | collective-permute-start | bytes 442376 | tf_op jit(solution)/shard_map/while/body/eval_jaxpr/ppermute | solution.py:17
  120.2 11.5 %collective-permute-start = (bf16[128,576]{0,1:T(8,128)(2,1)}, bf16[128,576]{0,1:T(8,128)(2,1)S(1)}, u32[]{:S(2)}, u32[]{:S(2)}) collective-permute-start(bf16[128,576]{0,1:T(8,128)(2,1)} %get-tuple-element.429), channel_id=1, source_target_pairs={{248,0},{0,8},{8,16},{16,24},{24,32},{32,40},{40,48},{48,56},{56,6... | collective-permute-start | bytes 442376 | tf_op jit(solution)/shard_map/while/body/eval_jaxpr/ppermute | solution.py:17
  134.2 11.5 %collective-permute-start = (bf16[128,576]{0,1:T(8,128)(2,1)}, bf16[128,576]{0,1:T(8,128)(2,1)S(1)}, u32[]{:S(2)}, u32[]{:S(2)}) collective-permute-start(bf16[128,576]{0,1:T(8,128)(2,1)} %get-tuple-element.429), channel_id=1, source_target_pairs={{248,0},{0,8},{8,16},{16,24},{24,32},{32,40},{40,48},{48,56},{56,6... | collective-permute-start | bytes 442376 | tf_op jit(solution)/shard_map/while/body/eval_jaxpr/ppermute | solution.py:17
  148.1 8.4 %collective-permute-start = (bf16[128,576]{0,1:T(8,128)(2,1)}, bf16[128,576]{0,1:T(8,128)(2,1)S(1)}, u32[]{:S(2)}, u32[]{:S(2)}) collective-permute-start(bf16[128,576]{0,1:T(8,128)(2,1)} %get-tuple-element.429), channel_id=1, source_target_pairs={{248,0},{0,8},{8,16},{16,24},{24,32},{32,40},{40,48},{48,56},{56,6... | collective-permute-start | bytes 442376 | tf_op jit(solution)/shard_map/while/body/eval_jaxpr/ppermute | solution.py:17
  159.0 8.4 %collective-permute-start = (bf16[128,576]{0,1:T(8,128)(2,1)}, bf16[128,576]{0,1:T(8,128)(2,1)S(1)}, u32[]{:S(2)}, u32[]{:S(2)}) collective-permute-start(bf16[128,576]{0,1:T(8,128)(2,1)} %get-tuple-element.429), channel_id=1, source_target_pairs={{248,0},{0,8},{8,16},{16,24},{24,32},{32,40},{40,48},{48,56},{56,6... | collective-permute-start | bytes 442376 | tf_op jit(solution)/shard_map/while/body/eval_jaxpr/ppermute | solution.py:17
  169.8 8.4 %collective-permute-start = (bf16[128,576]{0,1:T(8,128)(2,1)}, bf16[128,576]{0,1:T(8,128)(2,1)S(1)}, u32[]{:S(2)}, u32[]{:S(2)}) collective-permute-start(bf16[128,576]{0,1:T(8,128)(2,1)} %get-tuple-element.429), channel_id=1, source_target_pairs={{248,0},{0,8},{8,16},{16,24},{24,32},{32,40},{40,48},{48,56},{56,6... | collective-permute-start | bytes 442376 | tf_op jit(solution)/shard_map/while/body/eval_jaxpr/ppermute | solution.py:17
  180.6 8.4 %collective-permute-start = (bf16[128,576]{0,1:T(8,128)(2,1)}, bf16[128,576]{0,1:T(8,128)(2,1)S(1)}, u32[]{:S(2)}, u32[]{:S(2)}) collective-permute-start(bf16[128,576]{0,1:T(8,128)(2,1)} %get-tuple-element.429), channel_id=1, source_target_pairs={{248,0},{0,8},{8,16},{16,24},{24,32},{32,40},{40,48},{48,56},{56,6... | collective-permute-start | bytes 442376 | tf_op jit(solution)/shard_map/while/body/eval_jaxpr/ppermute | solution.py:17
  191.5 8.4 %collective-permute-start = (bf16[128,576]{0,1:T(8,128)(2,1)}, bf16[128,576]{0,1:T(8,128)(2,1)S(1)}, u32[]{:S(2)}, u32[]{:S(2)}) collective-permute-start(bf16[128,576]{0,1:T(8,128)(2,1)} %get-tuple-element.429), channel_id=1, source_target_pairs={{248,0},{0,8},{8,16},{16,24},{24,32},{32,40},{40,48},{48,56},{56,6... | collective-permute-start | bytes 442376 | tf_op jit(solution)/shard_map/while/body/eval_jaxpr/ppermute | solution.py:17
  202.3 8.4 %collective-permute-start = (bf16[128,576]{0,1:T(8,128)(2,1)}, bf16[128,576]{0,1:T(8,128)(2,1)S(1)}, u32[]{:S(2)}, u32[]{:S(2)}) collective-permute-start(bf16[128,576]{0,1:T(8,128)(2,1)} %get-tuple-element.429), channel_id=1, source_target_pairs={{248,0},{0,8},{8,16},{16,24},{24,32},{32,40},{40,48},{48,56},{56,6... | collective-permute-start | bytes 442376 | tf_op jit(solution)/shard_map/while/body/eval_jaxpr/ppermute | solution.py:17
  213.2 8.4 %collective-permute-start = (bf16[128,576]{0,1:T(8,128)(2,1)}, bf16[128,576]{0,1:T(8,128)(2,1)S(1)}, u32[]{:S(2)}, u32[]{:S(2)}) collective-permute-start(bf16[128,576]{0,1:T(8,128)(2,1)} %get-tuple-element.429), channel_id=1, source_target_pairs={{248,0},{0,8},{8,16},{16,24},{24,32},{32,40},{40,48},{48,56},{56,6... | collective-permute-start | bytes 442376 | tf_op jit(solution)/shard_map/while/body/eval_jaxpr/ppermute | solution.py:17
  224.0 8.4 %collective-permute-start = (bf16[128,576]{0,1:T(8,128)(2,1)}, bf16[128,576]{0,1:T(8,128)(2,1)S(1)}, u32[]{:S(2)}, u32[]{:S(2)}) collective-permute-start(bf16[128,576]{0,1:T(8,128)(2,1)} %get-tuple-element.429), channel_id=1, source_target_pairs={{248,0},{0,8},{8,16},{16,24},{24,32},{32,40},{40,48},{48,56},{56,6... | collective-permute-start | bytes 442376 | tf_op jit(solution)/shard_map/while/body/eval_jaxpr/ppermute | solution.py:17
  234.8 8.4 %collective-permute-start = (bf16[128,576]{0,1:T(8,128)(2,1)}, bf16[128,576]{0,1:T(8,128)(2,1)S(1)}, u32[]{:S(2)}, u32[]{:S(2)}) collective-permute-start(bf16[128,576]{0,1:T(8,128)(2,1)} %get-tuple-element.429), channel_id=1, source_target_pairs={{248,0},{0,8},{8,16},{16,24},{24,32},{32,40},{40,48},{48,56},{56,6... | collective-permute-start | bytes 442376 | tf_op jit(solution)/shard_map/while/body/eval_jaxpr/ppermute | solution.py:17
  245.7 8.4 %collective-permute-start = (bf16[128,576]{0,1:T(8,128)(2,1)}, bf16[128,576]{0,1:T(8,128)(2,1)S(1)}, u32[]{:S(2)}, u32[]{:S(2)}) collective-permute-start(bf16[128,576]{0,1:T(8,128)(2,1)} %get-tuple-element.429), channel_id=1, source_target_pairs={{248,0},{0,8},{8,16},{16,24},{24,32},{32,40},{40,48},{48,56},{56,6... | collective-permute-start | bytes 442376 | tf_op jit(solution)/shard_map/while/body/eval_jaxpr/ppermute | solution.py:17
  256.5 8.4 %collective-permute-start = (bf16[128,576]{0,1:T(8,128)(2,1)}, bf16[128,576]{0,1:T(8,128)(2,1)S(1)}, u32[]{:S(2)}, u32[]{:S(2)}) collective-permute-start(bf16[128,576]{0,1:T(8,128)(2,1)} %get-tuple-element.429), channel_id=1, source_target_pairs={{248,0},{0,8},{8,16},{16,24},{24,32},{32,40},{40,48},{48,56},{56,6... | collective-permute-start | bytes 442376 | tf_op jit(solution)/shard_map/while/body/eval_jaxpr/ppermute | solution.py:17
  267.3 8.4 %collective-permute-start = (bf16[128,576]{0,1:T(8,128)(2,1)}, bf16[128,576]{0,1:T(8,128)(2,1)S(1)}, u32[]{:S(2)}, u32[]{:S(2)}) collective-permute-start(bf16[128,576]{0,1:T(8,128)(2,1)} %get-tuple-element.429), channel_id=1, source_target_pairs={{248,0},{0,8},{8,16},{16,24},{24,32},{32,40},{40,48},{48,56},{56,6... | collective-permute-start | bytes 442376 | tf_op jit(solution)/shard_map/while/body/eval_jaxpr/ppermute | solution.py:17
  278.2 8.4 %collective-permute-start = (bf16[128,576]{0,1:T(8,128)(2,1)}, bf16[128,576]{0,1:T(8,128)(2,1)S(1)}, u32[]{:S(2)}, u32[]{:S(2)}) collective-permute-start(bf16[128,576]{0,1:T(8,128)(2,1)} %get-tuple-element.429), channel_id=1, source_target_pairs={{248,0},{0,8},{8,16},{16,24},{24,32},{32,40},{40,48},{48,56},{56,6... | collective-permute-start | bytes 442376 | tf_op jit(solution)/shard_map/while/body/eval_jaxpr/ppermute | solution.py:17
  289.0 8.4 %collective-permute-start = (bf16[128,576]{0,1:T(8,128)(2,1)}, bf16[128,576]{0,1:T(8,128)(2,1)S(1)}, u32[]{:S(2)}, u32[]{:S(2)}) collective-permute-start(bf16[128,576]{0,1:T(8,128)(2,1)} %get-tuple-element.429), channel_id=1, source_target_pairs={{248,0},{0,8},{8,16},{16,24},{24,32},{32,40},{40,48},{48,56},{56,6... | collective-permute-start | bytes 442376 | tf_op jit(solution)/shard_map/while/body/eval_jaxpr/ppermute | solution.py:17
  299.9 8.4 %collective-permute-start = (bf16[128,576]{0,1:T(8,128)(2,1)}, bf16[128,576]{0,1:T(8,128)(2,1)S(1)}, u32[]{:S(2)}, u32[]{:S(2)}) collective-permute-start(bf16[128,576]{0,1:T(8,128)(2,1)} %get-tuple-element.429), channel_id=1, source_target_pairs={{248,0},{0,8},{8,16},{16,24},{24,32},{32,40},{40,48},{48,56},{56,6... | collective-permute-start | bytes 442376 | tf_op jit(solution)/shard_map/while/body/eval_jaxpr/ppermute | solution.py:17
  310.7 8.4 %collective-permute-start = (bf16[128,576]{0,1:T(8,128)(2,1)}, bf16[128,576]{0,1:T(8,128)(2,1)S(1)}, u32[]{:S(2)}, u32[]{:S(2)}) collective-permute-start(bf16[128,576]{0,1:T(8,128)(2,1)} %get-tuple-element.429), channel_id=1, source_target_pairs={{248,0},{0,8},{8,16},{16,24},{24,32},{32,40},{40,48},{48,56},{56,6... | collective-permute-start | bytes 442376 | tf_op jit(solution)/shard_map/while/body/eval_jaxpr/ppermute | solution.py:17
  321.5 8.4 %collective-permute-start = (bf16[128,576]{0,1:T(8,128)(2,1)}, bf16[128,576]{0,1:T(8,128)(2,1)S(1)}, u32[]{:S(2)}, u32[]{:S(2)}) collective-permute-start(bf16[128,576]{0,1:T(8,128)(2,1)} %get-tuple-element.429), channel_id=1, source_target_pairs={{248,0},{0,8},{8,16},{16,24},{24,32},{32,40},{40,48},{48,56},{56,6... | collective-permute-start | bytes 442376 | tf_op jit(solution)/shard_map/while/body/eval_jaxpr/ppermute | solution.py:17
  332.4 8.4 %collective-permute-start = (bf16[128,576]{0,1:T(8,128)(2,1)}, bf16[128,576]{0,1:T(8,128)(2,1)S(1)}, u32[]{:S(2)}, u32[]{:S(2)}) collective-permute-start(bf16[128,576]{0,1:T(8,128)(2,1)} %get-tuple-element.429), channel_id=1, source_target_pairs={{248,0},{0,8},{8,16},{16,24},{24,32},{32,40},{40,48},{48,56},{56,6... | collective-permute-start | bytes 442376 | tf_op jit(solution)/shard_map/while/body/eval_jaxpr/ppermute | solution.py:17
  343.2 8.4 %collective-permute-start = (bf16[128,576]{0,1:T(8,128)(2,1)}, bf16[128,576]{0,1:T(8,128)(2,1)S(1)}, u32[]{:S(2)}, u32[]{:S(2)}) collective-permute-start(bf16[128,576]{0,1:T(8,128)(2,1)} %get-tuple-element.429), channel_id=1, source_target_pairs={{248,0},{0,8},{8,16},{16,24},{24,32},{32,40},{40,48},{48,56},{56,6... | collective-permute-start | bytes 442376 | tf_op jit(solution)/shard_map/while/body/eval_jaxpr/ppermute | solution.py:17
  354.1 8.4 %collective-permute-start = (bf16[128,576]{0,1:T(8,128)(2,1)}, bf16[128,576]{0,1:T(8,128)(2,1)S(1)}, u32[]{:S(2)}, u32[]{:S(2)}) collective-permute-start(bf16[128,576]{0,1:T(8,128)(2,1)} %get-tuple-element.429), channel_id=1, source_target_pairs={{248,0},{0,8},{8,16},{16,24},{24,32},{32,40},{40,48},{48,56},{56,6... | collective-permute-start | bytes 442376 | tf_op jit(solution)/shard_map/while/body/eval_jaxpr/ppermute | solution.py:17
  364.9 8.4 %collective-permute-start = (bf16[128,576]{0,1:T(8,128)(2,1)}, bf16[128,576]{0,1:T(8,128)(2,1)S(1)}, u32[]{:S(2)}, u32[]{:S(2)}) collective-permute-start(bf16[128,576]{0,1:T(8,128)(2,1)} %get-tuple-element.429), channel_id=1, source_target_pairs={{248,0},{0,8},{8,16},{16,24},{24,32},{32,40},{40,48},{48,56},{56,6... | collective-permute-start | bytes 442376 | tf_op jit(solution)/shard_map/while/body/eval_jaxpr/ppermute | solution.py:17
  386.6 8.4 %collective-permute-start = (bf16[128,576]{0,1:T(8,128)(2,1)}, bf16[128,576]{0,1:T(8,128)(2,1)S(1)}, u32[]{:S(2)}, u32[]{:S(2)}) collective-permute-start(bf16[128,576]{0,1:T(8,128)(2,1)} %get-tuple-element.429), channel_id=1, source_target_pairs={{248,0},{0,8},{8,16},{16,24},{24,32},{32,40},{40,48},{48,56},{56,6... | collective-permute-start | bytes 442376 | tf_op jit(solution)/shard_map/while/body/eval_jaxpr/ppermute | solution.py:17
  397.4 8.4 %collective-permute-start = (bf16[128,576]{0,1:T(8,128)(2,1)}, bf16[128,576]{0,1:T(8,128)(2,1)S(1)}, u32[]{:S(2)}, u32[]{:S(2)}) collective-permute-start(bf16[128,576]{0,1:T(8,128)(2,1)} %get-tuple-element.429), channel_id=1, source_target_pairs={{248,0},{0,8},{8,16},{16,24},{24,32},{32,40},{40,48},{48,56},{56,6... | collective-permute-start | bytes 442376 | tf_op jit(solution)/shard_map/while/body/eval_jaxpr/ppermute | solution.py:17
  (4 other events, 21.5 us)
Sparse Core Ops, SparseCore 0:
  10.1 135.7 all-gather.2
  421.2 41.0 reduce-scatter.3
where the time goes:
time: 474 us; the launch traced here: 471 us
  waiting for transfers between devices  264 us (56%)
  matrix products  60 us (13%)
  local copies, waits for them, and re-layouts  56.4 us (12%)
  blocking collectives  43.7 us (9%)
  other arithmetic  30.3 us (6%)
  between operations  13.6 us (3%)
    ppermute x31, waiting for transfers between devices, shifted(): return lax.ppermute(block, axis, route)  222 us
    all_gather x1, blocking collectives, local(): all_positions = lax.all_gather(positions, 'seq', axis=0, tiled=True)  43.7 us
    unnamed x3, waiting for transfers between devices  41.9 us
    while x93, local copies, waits for them, and re-layouts  24.1 us
    ge x32, other arithmetic, update(): visible = positions[:, None] >= key_pos[None, :]  23.6 us
    dynamic_slice x32, local copies, waits for them, and re-layouts, attend(): key_pos = lax.dynamic_slice_in_dim(all_positions, anchor * width, width)  23.3 us
    dot_general x32, matrix products, update(): jnp.dot(block[:, :KV_RANK], kv_up, preferred_element_type=jnp.float32)  16.7 us
    dot_general x32, matrix products, update(): jnp.einsum('hij,jhd->hid', expo.astype(jnp.bfloat16), keys_values[:, :, N...  13.5 us
  transfers between devices with their start and end apart: 33, of which 32 were waited for; matrix products, arithmetic and copies ran while one was open for 28% of the time, Pallas kernels for 0%

commit v1 on v0

v1 whole, which is shorter than its diff:
```python
import functools
import math

import jax
import jax.numpy as jnp
from jax import lax
from jax.experimental import pallas as pl
from jax.experimental.pallas import tpu as pltpu
from jax.sharding import PartitionSpec as P

KV_RANK = 512
ROPE = 64
NOPE = 128
VDIM = 128
ROWS = 128
HEADS = 8
WIDE = 640
HIDDEN = -1e30
MESH = pl.DeviceIdType.MESH
F32 = jnp.float32
BF16 = jnp.bfloat16


def place():
    s, h = lax.axis_index("seq"), lax.axis_index("head")
    return s // 4, lax.rem(s // 2, 2), lax.rem(s, 2), h // 4, lax.rem(h, 4)


def at(z, xh, c, xl, y):
    return (lax.rem(z + 8, 8) * 4 + xh * 2 + c, xl * 4 + lax.rem(y + 4, 4))


def dot_nt(a, b):
    return lax.dot_general(a, b, (((1,), (1,)), ((), ())), preferred_element_type=F32)


def attention_kernel(
    pos_ref, lat_ref, gain_ref, qn_hbm, qr_hbm, up_hbm, att_ref,
    keys, qn, qr, up, query, top, total, summed,
    local_sem, x_send, x_recv, c_send, c_recv, z_send, z_recv, y_send, y_recv, d_send, d_recv,
):
    z, xh, c, xl, y = place()
    loads = [
        pltpu.make_async_copy(qn_hbm, qn, local_sem.at[0]),
        pltpu.make_async_copy(up_hbm, up, local_sem.at[1]),
        pltpu.make_async_copy(qr_hbm, qr, local_sem.at[2]),
    ]
    for load in loads:
        load.start()
    across = at(z, 1 - xh, c, 1 - xl, y)
    partner = at(z, xh, 1 - c, xl, y)
    right, left = at(z + 1, xh, c, xl, y), at(z - 1, xh, c, xl, y)
    above, below = at(z, xh, c, xl, y + 1), at(z, xh, c, xl, y - 1)
    barrier = pltpu.get_barrier_semaphore()
    for peer in (across, partner, right, left, above, below):
        pl.semaphore_signal(barrier, inc=1, device_id=peer, device_id_type=MESH)

    block_no = pos_ref[0] // ROWS
    lane = lax.broadcasted_iota(jnp.int32, (ROWS, 128), 1)
    coded = lat_ref[:, :KV_RANK].astype(F32)
    latent = coded * lax.rsqrt(jnp.mean(coded * coded, axis=1, keepdims=True) + 1e-06) * gain_ref[...]
    keys[z, xh, c, :, :KV_RANK] = latent.astype(BF16)
    rope = lat_ref[:, KV_RANK:].astype(F32)
    tail = jnp.concatenate([rope, jnp.zeros((ROWS, 64), F32)], axis=1)
    keys[z, xh, c, :, KV_RANK:] = jnp.where(lane == 64 + block_no, 1.0, tail).astype(BF16)
    pl.semaphore_wait(barrier, 6)

    half = pl.multiple_of(lax.rem(y, 2) * 64, 64)
    other = pl.multiple_of(64 - half, 64)
    half_hi = pl.multiple_of(half + 32, 32)
    other_hi = pl.multiple_of(other + 32, 32)

    def remote(ref, send, recv, peer):
        return pltpu.make_async_remote_copy(
            src_ref=ref, dst_ref=ref, send_sem=send, recv_sem=recv, device_id=peer, device_id_type=MESH
        )

    sent = []

    def push(ref, send, recv, peer):
        copy = remote(ref, send, recv, peer)
        copy.start()
        sent.append(copy)

    def landed(ref, send, recv):
        remote(ref, send, recv, partner).wait_recv()

    slab = lambda k: lax.rem(z + k + 8, 8)
    slots = {-1: 0, 1: 1, -2: 2, 2: 3, -3: 4, 3: 5, 4: 6}

    push(keys.at[z, xh, c, pl.ds(half, 64)], x_send.at[0], x_recv.at[0], across)
    push(keys.at[z, xh, c, pl.ds(other, 64)], x_send.at[1], x_recv.at[1], across)
    push(keys.at[z, xh, c], c_send.at[0], c_recv.at[0], partner)

    def prepare():
        loads[0].wait()
        loads[1].wait()
        loads[2].wait()
        ahead = jnp.where((lane >= 64) & (lane - 64 > block_no) & (lane < 96), HIDDEN, 0.0)
        for h in range(HEADS):
            rows = pl.ds(h * ROWS, ROWS)
            folded = dot_nt(qn[:, h * NOPE : (h + 1) * NOPE], up[:, h * 256 : h * 256 + NOPE])
            query[rows, :KV_RANK] = folded.astype(BF16)
            turned = qr[:, h * ROPE : (h + 1) * ROPE].astype(F32)
            turned = jnp.concatenate([turned, jnp.zeros((ROWS, 64), F32)], axis=1)
            query[rows, KV_RANK:] = (turned + ahead).astype(BF16)

    factor = math.log2(math.e) / math.sqrt(NOPE + ROPE)

    def attend(offsets, part, first=False):
        rows = pl.ds(part * 256, 256)
        q = query[rows, :]
        blocks = [keys[slab(k)].reshape(512, WIDE) for k in offsets]
        scores = [dot_nt(q, block) for block in blocks]
        if first:
            own = xh * 256 + c * ROWS
            token = lax.rem(lax.broadcasted_iota(jnp.int32, (256, 512), 0), ROWS)
            ahead = lax.broadcasted_iota(jnp.int32, (256, 512), 1) - own
            scores[0] = jnp.where((ahead > token) & (ahead < ROWS), HIDDEN, scores[0])
        most = functools.reduce(jnp.maximum, [jnp.max(s, axis=1, keepdims=True) for s in scores])
        if not first:
            before = top[rows, :1]
            most = jnp.maximum(most, before)
            fade = jnp.exp2((before - most) * factor)
        adds, totals = [], []
        for s, block in zip(scores, blocks):
            expo = jnp.exp2((s - most) * factor)
            for i in range(4):
                totals.append(expo[:, i * 128 : (i + 1) * 128])
            adds.append(jnp.dot(expo.astype(BF16), block[:, :KV_RANK], preferred_element_type=F32))
        gain = functools.reduce(jnp.add, adds)
        mass = functools.reduce(jnp.add, totals)
        if first:
            summed[rows, :] = gain
            total[rows, :] = mass
        else:
            summed[rows, :] = summed[rows, :] * fade + gain
            total[rows, :] = total[rows, :] * fade + mass
        top[rows, :] = jnp.broadcast_to(most, (256, 128))

    def from_z(d):
        for k, way, forward in ((-d, 0, right), (d, 1, left)):
            if d < 4:
                ref = keys.at[slab(k), :, c, pl.ds(half, 64)]
                landed(ref, z_send.at[way, d - 1], z_recv.at[way, d - 1])
                if d < 3:
                    push(ref, z_send.at[way, d], z_recv.at[way, d], forward)
                else:
                    push(keys.at[slab(k), way, c, pl.ds(half, 64)], z_send.at[way, 3], z_recv.at[way, 3], forward)
            else:
                landed(keys.at[slab(4), way, c, pl.ds(half, 64)], z_send.at[way, 3], z_recv.at[way, 3])
        for k in (-d, d) if d < 4 else (4,):
            i = slots[k]
            push(keys.at[slab(k), :, c, pl.ds(half, 32)], y_send.at[0, i], y_recv.at[0, i], above)
            push(keys.at[slab(k), :, c, pl.ds(half_hi, 32)], y_send.at[1, i], y_recv.at[1, i], below)
            push(keys.at[slab(k), :, c, pl.ds(half, 64)], d_send.at[0, i], d_recv.at[0, i], partner)

    def from_y(d):
        for k in (-d, d) if d < 4 else (4,):
            i = slots[k]
            landed(keys.at[slab(k), :, c, pl.ds(other, 32)], y_send.at[0, i], y_recv.at[0, i])
            landed(keys.at[slab(k), :, c, pl.ds(other_hi, 32)], y_send.at[1, i], y_recv.at[1, i])
            push(keys.at[slab(k), :, c, pl.ds(other, 64)], d_send.at[1, i], d_recv.at[1, i], partner)

    def ready(d):
        for k in (-d, d) if d < 4 else (4,):
            i = slots[k]
            landed(keys.at[slab(k), :, 1 - c, pl.ds(half, 64)], d_send.at[0, i], d_recv.at[0, i])
            landed(keys.at[slab(k), :, 1 - c, pl.ds(other, 64)], d_send.at[1, i], d_recv.at[1, i])

    prepare()
    landed(keys.at[z, 1 - xh, c, pl.ds(half, 64)], x_send.at[0], x_recv.at[0])
    start = keys.at[z, :, c, pl.ds(half, 64)]
    push(start, z_send.at[0, 0], z_recv.at[0, 0], right)
    push(start, z_send.at[1, 0], z_recv.at[1, 0], left)
    landed(keys.at[z, 1 - xh, c, pl.ds(other, 64)], x_send.at[1], x_recv.at[1])
    push(keys.at[z, 1 - xh, c], c_send.at[1], c_recv.at[1], partner)
    landed(keys.at[z, xh, 1 - c], c_send.at[0], c_recv.at[0])
    landed(keys.at[z, 1 - xh, 1 - c], c_send.at[1], c_recv.at[1])
    for part in range(4):
        attend((0,), part, first=True)
    from_z(1)
    from_y(1)
    ready(1)
    from_z(2)
    for part in range(4):
        attend((-1, 1), part)
        if part == 1:
            from_y(2)
        if part == 2:
            from_z(3)
    ready(2)
    for part in range(4):
        attend((-2, 2), part)
        if part == 0:
            from_y(3)
        if part == 1:
            from_z(4)
    ready(3)
    for part in range(4):
        attend((-3, 3), part)
        if part == 1:
            from_y(4)
    ready(4)
    for part in range(4):
        attend((4,), part)
    for h in range(HEADS):
        rows = pl.ds(h * ROWS, ROWS)
        share = summed[rows, :] / jnp.sum(total[rows, :], axis=1, keepdims=True)
        value = jnp.dot(share.astype(BF16), up[:, h * 256 + NOPE : (h + 1) * 256], preferred_element_type=F32)
        att_ref[:, h * VDIM : (h + 1) * VDIM] = value.astype(BF16)
    for copy in sent:
        copy.wait_send()


def attention(positions, kv_latent, gain, q_nope, q_rope, kv_up):
    dma = pltpu.SemaphoreType.DMA
    vmem, smem, any_ = (pl.BlockSpec(memory_space=m) for m in (pltpu.VMEM, pltpu.SMEM, pl.ANY))
    return pl.pallas_call(
        attention_kernel,
        out_shape=jax.ShapeDtypeStruct((ROWS, HEADS * VDIM), BF16),
        in_specs=[smem, vmem, vmem, any_, any_, any_],
        out_specs=vmem,
        scratch_shapes=[
            pltpu.VMEM((8, 2, 2, ROWS, WIDE), BF16),
            pltpu.VMEM((ROWS, HEADS * NOPE), BF16),
            pltpu.VMEM((ROWS, HEADS * ROPE), BF16),
            pltpu.VMEM((KV_RANK, HEADS * 256), BF16),
            pltpu.VMEM((HEADS * ROWS, WIDE), BF16),
            pltpu.VMEM((HEADS * ROWS, 128), F32),
            pltpu.VMEM((HEADS * ROWS, 128), F32),
            pltpu.VMEM((HEADS * ROWS, KV_RANK), F32),
            dma((3,)), dma((2,)), dma((2,)), dma((2,)), dma((2,)),
            dma((2, 4)), dma((2, 4)), dma((2, 7)), dma((2, 7)), dma((2, 7)), dma((2, 7)),
        ],
        compiler_params=pltpu.CompilerParams(
            collective_id=0, has_side_effects=True, vmem_limit_bytes=48 * 2**20
        ),
        cost_estimate=pl.CostEstimate(flops=11 * 10**9, bytes_accessed=4 * 10**6, transcendentals=4 * 10**6),
        name="attention",
    )(positions, kv_latent, gain, q_nope, q_rope, kv_up)


def project_kernel(
    att_ref, w_hbm, out_ref, held, w, part, reached, half_sum, final,
    w_sem, a_send, a_recv, y_send, y_recv, f_send, f_recv,
):
    z, xh, c, xl, y = place()
    head = xl * 4 + y
    load = pltpu.make_async_copy(w_hbm, w, w_sem)
    load.start()
    right, left = at(z + 1, xh, c, xl, y), at(z - 1, xh, c, xl, y)
    barrier = pltpu.get_barrier_semaphore()

    def greet(peer):
        pl.semaphore_signal(barrier, inc=1, device_id=peer, device_id_type=MESH)

    greet(right)
    greet(left)
    for j in (1, 2, 3):
        greet(at(z, xh, c, xl, y + j))
    for j in (0, 1):
        pl.when((head != z) | (xl != j))(lambda: greet(at(head, xh, c, j, lax.rem(z, 4))))
    pl.semaphore_wait(barrier, jnp.where(head == z, 6, 7))

    def remote(src, dst, send, recv, peer):
        return pltpu.make_async_remote_copy(
            src_ref=src, dst_ref=dst, send_sem=send, recv_sem=recv, device_id=peer, device_id_type=MESH
        )

    sent = []

    def push(src, dst, send, recv, peer):
        copy = remote(src, dst, send, recv, peer)
        copy.start()
        sent.append(copy)

    slab = lambda k: lax.rem(z + k + 8, 8)
    push(att_ref, held.at[z], a_send.at[0, 0], a_recv.at[0, 0], right)
    push(att_ref, held.at[z], a_send.at[1, 0], a_recv.at[1, 0], left)
    load.wait()
    order = (0, -1, 1, -2, 2, -3, 3, 4)

    def spread(i):
        block = slab(order[i])
        peer = at(z, xh, c, xl, lax.rem(block, 4))
        return remote(part.at[block], reached.at[block // 4, y], y_send.at[i], y_recv.at[block // 4, y], peer)

    def multiply(i):
        block = slab(order[i])
        a = att_ref[...] if i == 0 else held[block]
        part[block] = jnp.dot(a, w[...], preferred_element_type=F32).astype(BF16)
        pl.when(lax.rem(block, 4) != y)(lambda: spread(i).start())

    def collect(i):
        block = slab(order[i])
        k = block // 4

        @pl.when(lax.rem(block, 4) == y)
        def _():
            acc = part[block].astype(F32)
            for j in (1, 2, 3):
                who = lax.rem(y + j, 4)
                remote(part.at[block], reached.at[k, who], y_send.at[i], y_recv.at[k, who], right).wait_recv()
                acc = acc + reached[k, who].astype(F32)
            half_sum[k] = acc.astype(BF16)

            @pl.when((block == z) & (head == z))
            def _():
                pltpu.make_async_copy(half_sum.at[k], final.at[xl], f_recv.at[xl]).start()

            @pl.when((block != z) | (head != z))
            def _():
                peer = at(block, xh, c, z // 4, lax.rem(z, 4))
                remote(half_sum.at[k], final.at[xl], f_send.at[k], f_recv.at[xl], peer).start()

    multiply(0)
    for d in (1, 2, 3):
        for k, way, forward in ((-d, 0, right), (d, 1, left)):
            ref = held.at[slab(k)]
            remote(ref, ref, a_send.at[way, d - 1], a_recv.at[way, d - 1], right).wait_recv()
            if d < 3:
                push(ref, ref, a_send.at[way, d], a_recv.at[way, d], forward)
            else:
                piece = held.at[slab(k), pl.ds(way * 64, 64)]
                push(piece, piece, a_send.at[way, 3], a_recv.at[way, 3], forward)
        multiply(2 * d - 1)
        multiply(2 * d)
        if d == 1:
            collect(0)
        else:
            collect(2 * d - 3)
            collect(2 * d - 2)
    for way in (0, 1):
        piece = held.at[slab(4), pl.ds(way * 64, 64)]
        remote(piece, piece, a_send.at[way, 3], a_recv.at[way, 3], right).wait_recv()
    multiply(7)
    collect(5)
    collect(6)
    collect(7)
    for j in (0, 1):
        remote(half_sum.at[0], final.at[j], f_send.at[0], f_recv.at[j], right).wait_recv()
    out_ref[...] = (final[0].astype(F32) + final[1].astype(F32)).astype(BF16)
    for copy in sent:
        copy.wait_send()
    for i in range(8):
        pl.when(lax.rem(slab(order[i]), 4) != y)(lambda: spread(i).wait_send())
    for k in (0, 1):
        block = y + 4 * k

        @pl.when((block != z) | (head != z))
        def _():
            remote(half_sum.at[k], final.at[xl], f_send.at[k], f_recv.at[xl], right).wait_send()


def project(att, w):
    dma = pltpu.SemaphoreType.DMA
    vmem, any_ = (pl.BlockSpec(memory_space=m) for m in (pltpu.VMEM, pl.ANY))
    columns = w.shape[1]
    return pl.pallas_call(
        project_kernel,
        out_shape=jax.ShapeDtypeStruct((ROWS, columns), BF16),
        in_specs=[vmem, any_],
        out_specs=vmem,
        scratch_shapes=[
            pltpu.VMEM((8, ROWS, HEADS * VDIM), BF16),
            pltpu.VMEM((HEADS * VDIM, columns), BF16),
            pltpu.VMEM((8, ROWS, columns), BF16),
            pltpu.VMEM((2, 4, ROWS, columns), BF16),
            pltpu.VMEM((2, ROWS, columns), BF16),
            pltpu.VMEM((2, ROWS, columns), BF16),
            dma(()), dma((2, 4)), dma((2, 4)), dma((8,)), dma((2, 4)), dma((2,)), dma((2,)),
        ],
        compiler_params=pltpu.CompilerParams(
            collective_id=1, has_side_effects=True, vmem_limit_bytes=48 * 2**20
        ),
        cost_estimate=pl.CostEstimate(flops=2 * 10**9, bytes_accessed=4 * 10**6, transcendentals=0),
        name="project",
    )(att, w)


def local(q_nope, q_rope, kv_latent, positions, kv_gain, kv_up, w_out):
    groups = [[4 * z + i for i in range(4)] for z in range(8)]
    w = lax.all_gather(w_out, "seq", axis=1, tiled=True, axis_index_groups=groups)
    att = attention(positions, kv_latent, kv_gain.reshape(1, KV_RANK), q_nope, q_rope, kv_up)
    return project(att, w)


def solution(mesh):
    return jax.shard_map(
        local,
        mesh=mesh,
        in_specs=(
            P("seq", "head"),
            P("seq", "head"),
            P("seq", None),
            P("seq"),
            P(),
            P(None, "head"),
            P("head", "seq"),
        ),
        out_specs=P("seq", "head"),
        check_vma=False,
    )
```

time: 474 us -> 138 us (0.29)
  waiting for transfers between devices: 264 us -> 0.73 us
  Pallas kernels: 0 us -> 114 us
  matrix products: 60 us -> 0 us
  local copies, waits for them, and re-layouts: 56.4 us -> 9.59 us
  blocking collectives: 43.7 us -> 0 us
  other arithmetic: 30.3 us -> 0 us
    ppermute x31 -> x0, waiting for transfers between devices: 222 us -> none  [shifted(): return lax.ppermute(block, axis, route)]
    pallas_call x0 -> x2, Pallas kernels: none -> 114 us  [the longest x1 63.9 us: project(): pl.pallas_call(project_kernel, out_shape=jax.ShapeDtypeStruct((ROWS, colu...]
    dot_general x129 -> x0, matrix products: 60 us -> none  [the longest x32 16.7 us: update(): jnp.dot(block[:, :KV_RANK], kv_up, preferred_element_type=jnp.float32)]
    all_gather x1 -> x0, blocking collectives: 43.7 us -> none  [local(): all_positions = lax.all_gather(positions, 'seq', axis=0, tiled=True)]
    unnamed x3 -> x1, waiting for transfers between devices: 41.9 us -> 0.71 us
    while x95 -> x0, local copies, waits for them, and re-layouts: 24.4 us -> none
    ge x32 -> x0, other arithmetic: 23.6 us -> none  [update(): visible = positions[:, None] >= key_pos[None, :]]
    dynamic_slice x32 -> x0, local copies, waits for them, and re-layouts: 23.3 us -> none  [attend(): key_pos = lax.dynamic_slice_in_dim(all_positions, anchor * width, width)]
  transfers between devices with their start and end apart: 33 -> 1, of which waited for: 32 -> 0; matrix products, arithmetic and copies ran while one was open for 28% -> 1% of each run, Pallas kernels for 0% -> 36%
where the time goes in v1:
time: 138 us
  Pallas kernels  114 us (83%)
  between operations  13.4 us (10%)
  local copies, waits for them, and re-layouts  9.59 us (7%)
    pallas_call x1, Pallas kernels, project(): pl.pallas_call(project_kernel, out_shape=jax.ShapeDtypeStruct((ROWS, colu...  63.9 us
    pallas_call x1, Pallas kernels, attention(): pl.pallas_call(attention_kernel, out_shape=jax.ShapeDtypeStruct((ROWS, HE...  50.2 us
    unnamed x12, local copies, waits for them, and re-layouts  6.53 us
    all_gather x1, local copies, waits for them, and re-layouts, local(): lax.all_gather(w_out, 'seq', axis=1, tiled=True, axis_index_groups=groups)  3.06 us
  transfers between devices with their start and end apart: 1, of which 0 were waited for; matrix products, arithmetic and copies ran while one was open for 1% of the time, Pallas kernels for 36%

profile of v1, /device:TPU:2, one launch (start us, length us, event | category | flops | bytes accessed | tf_op | source)
XLA Modules:
  0.0 137.9 jit_solution(7867831919941413853)
XLA Ops:
  6.5 0.0 all-gather.2.cloned.1.call-start
  6.5 0.7 all-gather.2.cloned.1.call-update
  7.3 1.1 copy.10.lat_ref
  8.3 0.0 copy-start
  8.3 1.6 %copy-done = bf16[512,2048]{1,0:T(8,128)(2,1)S(1)} copy-done((bf16[512,2048]{1,0:T(8,128)(2,1)S(1)}, bf16[512,2048]{1,0:T(8,128)(2,1)}, u32[]{:S(2)}) %copy-start) | copy-done | bytes 2097176
  9.9 0.0 copy-start.1
  9.9 0.9 copy-done.1
  10.9 0.0 copy-start.2
  10.9 0.9 copy-done.2
  11.8 0.0 copy-start.3
  11.8 0.7 copy-done.3
  12.5 0.0 copy-start.4
  12.5 0.7 copy-done.4
  13.1 50.2 %attention.1.att_ref = bf16[128,1024]{1,0:T(8,128)(2,1)S(1)} custom-call(s32[128]{0:T(128)S(1)} %copy-done.4, bf16[128,576]{1,0:T(8,128)(2,1)S(1)} %copy.10.lat_ref, f32[1,512]{1,0:T(1,128)S(1)} %bitcast.1, bf16[128,1024]{1,0:T(8,128)(2,1)S(1)} %copy-done.1, bf16[128,512]{1,0:T(8,128)(2,1)S(1)} %copy-done.2, bf16[512,2048]{1,0:T(8,128)(2,1)S(1)} %copy-done), custom_call_target="tpu_custom_call" | custom-call | flops 11000000512 | bytes 4000000 | tf_op jit(solution)/shard_map/attention/pallas_call | solution.py:219
  63.4 0.0 all-gather.2.cloned.1.call-done
  63.4 3.1 %copy.11.w_hbm = bf16[1024,896]{1,0:T(8,128)(2,1)S(1)} copy(bf16[1024,896]{0,1:T(8,128)(2,1)} %all-gather.2.cloned.1.call-done) | data formatting | bytes 3670016 | tf_op jit(solution)/shard_map/all_gather | solution.py:384
  66.5 63.9 %project.1 = bf16[128,896]{1,0:T(8,128)(2,1)S(1)} custom-call(bf16[128,1024]{1,0:T(8,128)(2,1)S(1)} %attention.1.att_ref, bf16[1024,896]{1,0:T(8,128)(2,1)S(1)} %copy.11.w_hbm), custom_call_target="tpu_custom_call" | custom-call | flops 2000000000 | bytes 4000000 | tf_op jit(solution)/shard_map/project/pallas_call | solution.py:360
  130.4 0.7 copy.13
Async XLA Ops:
  6.5 56.8 %all-gather.2.cloned.1.call-start = ((), (), s32[]{:S(2)}) async-start(), calls=%async_computation | async-start | bytes 2293760 | tf_op jit(solution)/shard_map/all_gather | solution.py:384
  8.3 1.6 %copy-start = (bf16[512,2048]{1,0:T(8,128)(2,1)S(1)}, bf16[512,2048]{1,0:T(8,128)(2,1)}, u32[]{:S(2)}) copy-start(bf16[512,2048]{1,0:T(8,128)(2,1)} %up_hbm.1) | copy-start | bytes 6291460
  9.9 0.9 copy-start.1
  10.9 0.9 copy-start.2
  11.8 0.7 copy-start.3
  12.5 0.7 copy-start.4
Sparse Core Ops, SparseCore 0:
  9.2 29.7 all-gather.1

commit v2 on v1

--- a/solution.py
+++ b/solution.py
@@ -35,11 +35,18 @@
 
 
 def attention_kernel(
-    pos_ref, lat_ref, gain_ref, qn_hbm, qr_hbm, up_hbm, att_ref,
-    keys, qn, qr, up, query, top, total, summed,
+    pos_hbm, lat_hbm, gain_hbm, qn_hbm, qr_hbm, up_hbm, att_ref,
+    pos_ref, lat_ref, gain_ref, keys, qn, qr, up, query, top, total, summed,
     local_sem, x_send, x_recv, c_send, c_recv, z_send, z_recv, y_send, y_recv, d_send, d_recv,
 ):
     z, xh, c, xl, y = place()
+    first_loads = [
+        pltpu.make_async_copy(lat_hbm, lat_ref, local_sem.at[3]),
+        pltpu.make_async_copy(gain_hbm, gain_ref, local_sem.at[4]),
+        pltpu.make_async_copy(pos_hbm, pos_ref, local_sem.at[5]),
+    ]
+    for load in first_loads:
+        load.start()
     loads = [
         pltpu.make_async_copy(qn_hbm, qn, local_sem.at[0]),
         pltpu.make_async_copy(up_hbm, up, local_sem.at[1]),
@@ -55,13 +62,15 @@
     for peer in (across, partner, right, left, above, below):
         pl.semaphore_signal(barrier, inc=1, device_id=peer, device_id_type=MESH)
 
+    for load in first_loads:
+        load.wait()
     block_no = pos_ref[0] // ROWS
     lane = lax.broadcasted_iota(jnp.int32, (ROWS, 128), 1)
-    coded = lat_ref[:, :KV_RANK].astype(F32)
-    latent = coded * lax.rsqrt(jnp.mean(coded * coded, axis=1, keepdims=True) + 1e-06) * gain_ref[...]
+    coded = lat_ref[:KV_RANK, :].astype(F32).T
+    latent = coded * lax.rsqrt(jnp.mean(coded * coded, axis=1, keepdims=True) + 1e-06) * gain_ref[...].reshape(1, KV_RANK)
     keys[z, xh, c, :, :KV_RANK] = latent.astype(BF16)
-    rope = lat_ref[:, KV_RANK:].astype(F32)
-    tail = jnp.concatenate([rope, jnp.zeros((ROWS, 64), F32)], axis=1)
+    rope = lat_ref[KV_RANK:, :].astype(F32)
+    tail = jnp.concatenate([rope, jnp.zeros((64, ROWS), F32)], axis=0).T
     keys[z, xh, c, :, KV_RANK:] = jnp.where(lane == 64 + block_no, 1.0, tail).astype(BF16)
     pl.semaphore_wait(barrier, 6)
 
@@ -215,13 +224,16 @@
 
 def attention(positions, kv_latent, gain, q_nope, q_rope, kv_up):
     dma = pltpu.SemaphoreType.DMA
-    vmem, smem, any_ = (pl.BlockSpec(memory_space=m) for m in (pltpu.VMEM, pltpu.SMEM, pl.ANY))
+    vmem, any_ = (pl.BlockSpec(memory_space=m) for m in (pltpu.VMEM, pl.ANY))
     return pl.pallas_call(
         attention_kernel,
         out_shape=jax.ShapeDtypeStruct((ROWS, HEADS * VDIM), BF16),
-        in_specs=[smem, vmem, vmem, any_, any_, any_],
+        in_specs=[any_] * 6,
         out_specs=vmem,
         scratch_shapes=[
+            pltpu.SMEM((ROWS,), jnp.int32),
+            pltpu.VMEM((KV_RANK + ROPE, ROWS), BF16),
+            pltpu.VMEM((KV_RANK,), F32),
             pltpu.VMEM((8, 2, 2, ROWS, WIDE), BF16),
             pltpu.VMEM((ROWS, HEADS * NOPE), BF16),
             pltpu.VMEM((ROWS, HEADS * ROPE), BF16),
@@ -230,11 +242,11 @@
             pltpu.VMEM((HEADS * ROWS, 128), F32),
             pltpu.VMEM((HEADS * ROWS, 128), F32),
             pltpu.VMEM((HEADS * ROWS, KV_RANK), F32),
-            dma((3,)), dma((2,)), dma((2,)), dma((2,)), dma((2,)),
+            dma((6,)), dma((2,)), dma((2,)), dma((2,)), dma((2,)),
             dma((2, 4)), dma((2, 4)), dma((2, 7)), dma((2, 7)), dma((2, 7)), dma((2, 7)),
         ],
         compiler_params=pltpu.CompilerParams(
-            collective_id=0, has_side_effects=True, vmem_limit_bytes=48 * 2**20
+            collective_id=0, has_side_effects=True, vmem_limit_bytes=60 * 2**20
         ),
         cost_estimate=pl.CostEstimate(flops=11 * 10**9, bytes_accessed=4 * 10**6, transcendentals=4 * 10**6),
         name="attention",
@@ -242,8 +254,8 @@
 
 
 def project_kernel(
-    att_ref, w_hbm, out_ref, held, w, part, reached, half_sum, final,
-    w_sem, a_send, a_recv, y_send, y_recv, f_send, f_recv,
+    att_ref, w_hbm, out_ref, held, w, part, reached, done, final,
+    w_sem, a_send, a_recv, s_send, s_recv, f_send, f_recv,
 ):
     z, xh, c, xl, y = place()
     head = xl * 4 + y
@@ -251,17 +263,18 @@
     load.start()
     right, left = at(z + 1, xh, c, xl, y), at(z - 1, xh, c, xl, y)
     barrier = pltpu.get_barrier_semaphore()
+    seat = lambda plane, col: (lax.rem(plane, 8) * 4 + xh * 2 + c, lax.rem(col, 8))
 
     def greet(peer):
         pl.semaphore_signal(barrier, inc=1, device_id=peer, device_id_type=MESH)
 
     greet(right)
     greet(left)
-    for j in (1, 2, 3):
-        greet(at(z, xh, c, xl, y + j))
-    for j in (0, 1):
-        pl.when((head != z) | (xl != j))(lambda: greet(at(head, xh, c, j, lax.rem(z, 4))))
-    pl.semaphore_wait(barrier, jnp.where(head == z, 6, 7))
+    for j in range(1, 8):
+        greet(seat(z, head + j))
+    for j in range(8):
+        pl.when((head != z) | (head != j))(lambda: greet(seat(head, j)))
+    pl.semaphore_wait(barrier, jnp.where(head == z, 16, 17))
 
     def remote(src, dst, send, recv, peer):
         return pltpu.make_async_remote_copy(
@@ -276,87 +289,82 @@
         sent.append(copy)
 
     slab = lambda k: lax.rem(z + k + 8, 8)
-    push(att_ref, held.at[z], a_send.at[0, 0], a_recv.at[0, 0], right)
-    push(att_ref, held.at[z], a_send.at[1, 0], a_recv.at[1, 0], left)
+    for p in (0, 1):
+        piece = pl.ds(p * 64, 64)
+        push(att_ref.at[piece], held.at[z, piece], a_send.at[0, 0, p], a_recv.at[0, 0, p], right)
+        push(att_ref.at[piece], held.at[z, piece], a_send.at[1, 0, p], a_recv.at[1, 0, p], left)
     load.wait()
-    order = (0, -1, 1, -2, 2, -3, 3, 4)
-
-    def spread(i):
-        block = slab(order[i])
-        peer = at(z, xh, c, xl, lax.rem(block, 4))
-        return remote(part.at[block], reached.at[block // 4, y], y_send.at[i], y_recv.at[block // 4, y], peer)
-
-    def multiply(i):
-        block = slab(order[i])
-        a = att_ref[...] if i == 0 else held[block]
-        part[block] = jnp.dot(a, w[...], preferred_element_type=F32).astype(BF16)
-        pl.when(lax.rem(block, 4) != y)(lambda: spread(i).start())
-
-    def collect(i):
-        block = slab(order[i])
-        k = block // 4
-
-        @pl.when(lax.rem(block, 4) == y)
-        def _():
-            acc = part[block].astype(F32)
-            for j in (1, 2, 3):
-                who = lax.rem(y + j, 4)
-                remote(part.at[block], reached.at[k, who], y_send.at[i], y_recv.at[k, who], right).wait_recv()
-                acc = acc + reached[k, who].astype(F32)
-            half_sum[k] = acc.astype(BF16)
-
-            @pl.when((block == z) & (head == z))
+    own = pl.ds(pl.multiple_of(head * 16, 16), 16)
+
+    def multiply(k):
+        block = slab(k)
+        a = att_ref[...] if k == 0 else held[block]
+        part[block] = dot_nt(a, w[...]).astype(BF16)
+        for j in range(1, 8):
+            rows = pl.ds(pl.multiple_of(lax.rem(head + j, 8) * 16, 16), 16)
+            remote(
+                part.at[block, rows], reached.at[block, j - 1], s_send.at[block], s_recv.at[block], seat(z, head + j)
+            ).start()
+
+    def collect(k):
+        block = slab(k)
+        everything = reached.at[block]
+        remote(everything, everything, s_send.at[block], s_recv.at[block], right).wait_recv()
+        acc = part[block, own].astype(F32)
+        for j in range(7):
+            acc = acc + reached[block, j].astype(F32)
+        done[block] = acc.astype(BF16)
+        if k == 0:
+
+            @pl.when(head == z)
             def _():
-                pltpu.make_async_copy(half_sum.at[k], final.at[xl], f_recv.at[xl]).start()
-
-            @pl.when((block != z) | (head != z))
+                pltpu.make_async_copy(done.at[block], final.at[own], f_recv).start()
+
+            @pl.when(head != z)
             def _():
-                peer = at(block, xh, c, z // 4, lax.rem(z, 4))
-                remote(half_sum.at[k], final.at[xl], f_send.at[k], f_recv.at[xl], peer).start()
+                remote(done.at[block], final.at[own], f_send.at[0], f_recv, seat(block, z)).start()
+        else:
+            push(done.at[block], final.at[own], f_send.at[k + 3], f_recv, seat(block, z))
 
     multiply(0)
     for d in (1, 2, 3):
-        for k, way, forward in ((-d, 0, right), (d, 1, left)):
-            ref = held.at[slab(k)]
-            remote(ref, ref, a_send.at[way, d - 1], a_recv.at[way, d - 1], right).wait_recv()
-            if d < 3:
-                push(ref, ref, a_send.at[way, d], a_recv.at[way, d], forward)
-            else:
-                piece = held.at[slab(k), pl.ds(way * 64, 64)]
-                push(piece, piece, a_send.at[way, 3], a_recv.at[way, 3], forward)
-        multiply(2 * d - 1)
-        multiply(2 * d)
+        for p in (0, 1):
+            for k, way, forward in ((-d, 0, right), (d, 1, left)):
+                ref = held.at[slab(k), pl.ds(p * 64, 64)]
+                remote(ref, ref, a_send.at[way, d - 1, p], a_recv.at[way, d - 1, p], right).wait_recv()
+                if d < 3 or p == way:
+                    push(ref, ref, a_send.at[way, d, p], a_recv.at[way, d, p], forward)
+        multiply(-d)
+        multiply(d)
         if d == 1:
             collect(0)
         else:
-            collect(2 * d - 3)
-            collect(2 * d - 2)
+            collect(1 - d)
+            collect(d - 1)
     for way in (0, 1):
-        piece = held.at[slab(4), pl.ds(way * 64, 64)]
-        remote(piece, piece, a_send.at[way, 3], a_recv.at[way, 3], right).wait_recv()
-    multiply(7)
-    collect(5)
-    collect(6)
-    collect(7)
-    for j in (0, 1):
-        remote(half_sum.at[0], final.at[j], f_send.at[0], f_recv.at[j], right).wait_recv()
-    out_ref[...] = (final[0].astype(F32) + final[1].astype(F32)).astype(BF16)
+        ref = held.at[slab(4), pl.ds(way * 64, 64)]
+        remote(ref, ref, a_send.at[way, 3, way], a_recv.at[way, 3, way], right).wait_recv()
+    multiply(4)
+    collect(-3)
+    collect(3)
+    collect(4)
+    remote(final, final, f_send.at[0], f_recv, right).wait_recv()
+    out_ref[...] = final[...]
     for copy in sent:
         copy.wait_send()
-    for i in range(8):
-        pl.when(lax.rem(slab(order[i]), 4) != y)(lambda: spread(i).wait_send())
-    for k in (0, 1):
-        block = y + 4 * k
-
-        @pl.when((block != z) | (head != z))
-        def _():
-            remote(half_sum.at[k], final.at[xl], f_send.at[k], f_recv.at[xl], right).wait_send()
+    for block in range(8):
+        everything = reached.at[block]
+        remote(everything, everything, s_send.at[block], s_recv.at[block], right).wait_send()
+
+    @pl.when(head != z)
+    def _():
+        remote(done.at[0], done.at[0], f_send.at[0], f_recv, right).wait_send()
 
 
 def project(att, w):
     dma = pltpu.SemaphoreType.DMA
     vmem, any_ = (pl.BlockSpec(memory_space=m) for m in (pltpu.VMEM, pl.ANY))
-    columns = w.shape[1]
+    columns = w.shape[0]
     return pl.pallas_call(
         project_kernel,
         out_shape=jax.ShapeDtypeStruct((ROWS, columns), BF16),
@@ -364,15 +372,15 @@
         out_specs=vmem,
         scratch_shapes=[
             pltpu.VMEM((8, ROWS, HEADS * VDIM), BF16),
-            pltpu.VMEM((HEADS * VDIM, columns), BF16),
+            pltpu.VMEM(w.shape, BF16),
             pltpu.VMEM((8, ROWS, columns), BF16),
-            pltpu.VMEM((2, 4, ROWS, columns), BF16),
-            pltpu.VMEM((2, ROWS, columns), BF16),
-            pltpu.VMEM((2, ROWS, columns), BF16),
-            dma(()), dma((2, 4)), dma((2, 4)), dma((8,)), dma((2, 4)), dma((2,)), dma((2,)),
+            pltpu.VMEM((8, 7, 16, columns), BF16),
+            pltpu.VMEM((8, 16, columns), BF16),
+            pltpu.VMEM((ROWS, columns), BF16),
+            dma(()), dma((2, 4, 2)), dma((2, 4, 2)), dma((8,)), dma((8,)), dma((8,)), dma(()),
         ],
         compiler_params=pltpu.CompilerParams(
-            collective_id=1, has_side_effects=True, vmem_limit_bytes=48 * 2**20
+            collective_id=1, has_side_effects=True, vmem_limit_bytes=60 * 2**20
         ),
         cost_estimate=pl.CostEstimate(flops=2 * 10**9, bytes_accessed=4 * 10**6, transcendentals=0),
         name="project",
@@ -381,8 +389,8 @@
 
 def local(q_nope, q_rope, kv_latent, positions, kv_gain, kv_up, w_out):
     groups = [[4 * z + i for i in range(4)] for z in range(8)]
-    w = lax.all_gather(w_out, "seq", axis=1, tiled=True, axis_index_groups=groups)
-    att = attention(positions, kv_latent, kv_gain.reshape(1, KV_RANK), q_nope, q_rope, kv_up)
+    w = lax.all_gather(w_out.T, "seq", axis=0, tiled=True, axis_index_groups=groups)
+    att = attention(positions, kv_latent.T, kv_gain, q_nope, q_rope, kv_up)
     return project(att, w)
 
 

time: 138 us -> 113 us (0.82)
  Pallas kernels: 114 us -> 96.9 us
  local copies, waits for them, and re-layouts: 9.59 us -> 1.65 us
    pallas_call x1, Pallas kernels: 63.9 us -> 46.8 us  [project(): pl.pallas_call(project_kernel, out_shape=jax.ShapeDtypeStruct((ROWS, colu...]
    unnamed x12 -> x1, local copies, waits for them, and re-layouts: 6.53 us -> 1.65 us
    all_gather x1 -> x0, local copies, waits for them, and re-layouts: 3.06 us -> none  [local(): lax.all_gather(w_out, 'seq', axis=1, tiled=True, axis_index_groups=groups)]
  transfers between devices with their start and end apart: 1 -> 1, of which waited for: 0 -> 0; matrix products, arithmetic and copies ran while one was open for 1% -> 0% of each run, Pallas kernels for 36% -> 44%
where the time goes in v2:
time: 113 us
  Pallas kernels  96.9 us (86%)
  between operations  13.4 us (12%)
  local copies, waits for them, and re-layouts  1.65 us (1%)
    pallas_call x1, Pallas kernels, attention(): pl.pallas_call(attention_kernel, out_shape=jax.ShapeDtypeStruct((ROWS, HE...  50.1 us
    pallas_call x1, Pallas kernels, project(): pl.pallas_call(project_kernel, out_shape=jax.ShapeDtypeStruct((ROWS, colu...  46.8 us
  transfers between devices with their start and end apart: 1, of which 0 were waited for; matrix products, arithmetic and copies ran while one was open for 0% of the time, Pallas kernels for 44%

profile of v2, /device:TPU:2, one launch (start us, length us, event | category | flops | bytes accessed | tf_op | source)
XLA Modules:
  0.0 112.6 jit_solution(15205707937811173279)
XLA Ops:
  6.5 0.0 all-gather.2.cloned.1.call-start
  6.5 0.7 all-gather.2.cloned.1.call-update
  7.3 50.1 %attention.1.att_ref = bf16[128,1024]{1,0:T(8,128)(2,1)} custom-call(s32[128]{0:T(128)} %pos_hbm.1, bf16[576,128]{1,0:T(8,128)(2,1)} %bitcast.3, f32[512]{0:T(512)} %gain_hbm.1, bf16[128,1024]{1,0:T(8,128)(2,1)} %qn_hbm.1, bf16[128,512]{1,0:T(8,128)(2,1)} %qr_hbm.1, bf16[512,2048]{1,0:T(8,128)(2,1)} %up_hbm.1), custom_call_target="tpu_custom_call" | custom-call | flops 11000000512 | bytes 4000000 | tf_op jit(solution)/shard_map/attention/pallas_call | solution.py:228
  57.4 0.0 all-gather.2.cloned.1.call-done.w_hbm
  57.4 46.8 %project.1 = bf16[128,896]{1,0:T(8,128)(2,1)} custom-call(bf16[128,1024]{1,0:T(8,128)(2,1)} %attention.1.att_ref, bf16[896,1024]{1,0:T(8,128)(2,1)} %all-gather.2.cloned.1.call-done.w_hbm), custom_call_target="tpu_custom_call" | custom-call | flops 2000000000 | bytes 4000000 | tf_op jit(solution)/shard_map/project/pallas_call | solution.py:368
  104.2 1.6 %copy.9 = bf16[128,896]{1,0:T(8,128)(2,1)} copy(bf16[128,896]{1,0:T(8,128)(2,1)} %project.1) | data formatting | bytes 458752
Async XLA Ops:
  6.5 50.8 %all-gather.2.cloned.1.call-start = ((), (), s32[]{:S(2)}) async-start(), calls=%async_computation | async-start | bytes 2293760 | tf_op jit(solution)/shard_map/all_gather | solution.py:392
Sparse Core Ops, SparseCore 0:
  9.2 29.7 all-gather.1

commit v3 on v0

v3 whole, which is shorter than its diff:
```python
import math

import jax
import jax.numpy as jnp
from jax import lax
from jax.experimental import pallas as pl
from jax.experimental.pallas import tpu as pltpu
from jax.sharding import PartitionSpec as P

KV_RANK = 512
ROPE = 64
NOPE = 128
VDIM = 128
ROWS = 128
HEADS = 8
WIDE = 640
PART = 256
HIDDEN = -1e30
MESH = pl.DeviceIdType.MESH
F32 = jnp.float32
BF16 = jnp.bfloat16


def dot_nt(a, b):
    return lax.dot_general(a, b, (((1,), (1,)), ((), ())), preferred_element_type=F32)


def kernel(
    pos_hbm, lat_hbm, gain_hbm, qn_hbm, qr_hbm, up_hbm, w_hbm, out_ref,
    pos_ref, lat_ref, gain_ref, keys, qn, qr, up, query, top, total, summed,
    held, w, part, reached, done, final,
    local_sem, x_send, x_recv, c_send, c_recv, z_send, z_recv, n_send, n_recv, d_send, d_recv,
    w_send, w_recv, a_send, a_recv, s_send, s_recv, f_send, f_recv,
):
    s, head = lax.axis_index("seq"), lax.axis_index("head")
    z, xh, c, xl, y = s // 4, lax.rem(s // 2, 2), lax.rem(s, 2), head // 4, lax.rem(head, 4)

    def at(z, xh, c, xl, y):
        return (lax.rem(z + 8, 8) * 4 + xh * 2 + c, xl * 4 + lax.rem(y + 4, 4))

    def seat(plane, col):
        return (lax.rem(plane, 8) * 4 + xh * 2 + c, lax.rem(col, 8))

    def slab(k):
        return lax.rem(z + k + 8, 8)

    across, beside = at(z, 1 - xh, c, 1 - xl, y), at(z, xh, c, 1 - xl, y)
    partner, opposite = at(z, xh, 1 - c, xl, y), at(z, 1 - xh, c, xl, y)
    right, left = at(z + 1, xh, c, xl, y), at(z - 1, xh, c, xl, y)
    above, below = at(z, xh, c, xl, y + 1), at(z, xh, c, xl, y - 1)

    def remote(src, dst, send, recv, peer):
        return pltpu.make_async_remote_copy(
            src_ref=src, dst_ref=dst, send_sem=send, recv_sem=recv, device_id=peer, device_id_type=MESH
        )

    sent = []

    def push(src, dst, send, recv, peer):
        copy = remote(src, dst, send, recv, peer)
        copy.start()
        sent.append(copy)

    def landed(ref, send, recv):
        remote(ref, ref, send, recv, partner).wait_recv()

    def load(src, dst, i):
        copy = pltpu.make_async_copy(src, dst, local_sem.at[i])
        copy.start()
        return copy

    w_own = w.at[pl.ds(pl.multiple_of((xh * 2 + c) * 224, 32), 224)]
    first_loads = [load(lat_hbm, lat_ref, 0), load(gain_hbm, gain_ref, 1), load(pos_hbm, pos_ref, 2)]
    loads = [load(qn_hbm, qn, 3), load(up_hbm, up, 4), load(qr_hbm, qr, 5)]

    barrier = pltpu.get_barrier_semaphore()

    def greet(peer):
        pl.semaphore_signal(barrier, inc=1, device_id=peer, device_id_type=MESH)

    for peer in (across, partner, opposite, right, left):
        greet(peer)
    for j in range(1, 8):
        greet(seat(z, head + j))
    for j in range(8):
        pl.when((head != z) | (head != j))(lambda: greet(seat(head, j)))

    for copy in first_loads:
        copy.wait()
    block_no = pos_ref[0] // ROWS
    lane = lax.broadcasted_iota(jnp.int32, (ROWS, 128), 1)
    coded = lat_ref[:KV_RANK, :].astype(F32).T
    latent = coded * lax.rsqrt(jnp.mean(coded * coded, axis=1, keepdims=True) + 1e-06)
    keys[z, xh, c, :, :KV_RANK] = (latent * gain_ref[...].reshape(1, KV_RANK)).astype(BF16)
    rope = lat_ref[KV_RANK:, :].astype(F32)
    tail = jnp.concatenate([rope, jnp.zeros((64, ROWS), F32)], axis=0).T
    keys[z, xh, c, :, KV_RANK:] = jnp.where(lane == 64 + block_no, 1.0, tail).astype(BF16)
    pl.semaphore_wait(barrier, jnp.where(head == z, 19, 20))

    colour = lax.rem(2 * (2 * xh + xl) + y, 4)

    def quarter(i, start=0, size=32):
        return pl.ds(pl.multiple_of(lax.rem(colour + i, 4) * 32 + start, 16), size)

    push(keys.at[z, xh, c, quarter(2)], keys.at[z, xh, c, quarter(2)], x_send.at[0], x_recv.at[0], across)
    push(keys.at[z, xh, c], keys.at[z, xh, c], c_send.at[0], c_recv.at[0], partner)
    for i in (0, 1, 3):
        ref = keys.at[z, xh, c, quarter(i)]
        remote(ref, ref, x_send.at[1], x_recv.at[1], across).start()

    factor = math.log2(math.e) / math.sqrt(NOPE + ROPE)
    for copy in loads:
        copy.wait()
    ahead = jnp.where((lane >= 64) & (lane - 64 > block_no) & (lane < 96), HIDDEN, 0.0)
    for h in range(HEADS):
        rows = pl.ds(h * ROWS, ROWS)
        folded = dot_nt(qn[:, h * NOPE : (h + 1) * NOPE], up[:, h * 256 : h * 256 + NOPE])
        query[rows, :KV_RANK] = folded.astype(BF16)
        turned = qr[:, h * ROPE : (h + 1) * ROPE].astype(F32)
        turned = jnp.concatenate([turned, jnp.zeros((ROWS, 64), F32)], axis=1)
        query[rows, KV_RANK:] = (turned + ahead).astype(BF16)
        if h == 1:
            landed(keys.at[z, 1 - xh, c, quarter(0)], x_send.at[0], x_recv.at[0])
            start = keys.at[z, :, c, quarter(0)]
            push(start, start, z_send.at[0, 0], z_recv.at[0, 0], right)
            push(start, start, z_send.at[1, 0], z_recv.at[1, 0], left)

    def w_piece(i):
        piece = pl.ds(pl.multiple_of((xh * 2 + c) * 224 + i * 32, 32), 32)
        remote(w_hbm.at[pl.ds(i * 32, 32)], w.at[piece], w_send.at[0], w_recv.at[0], opposite).start()

    def scores_of(k, i):
        return dot_nt(query[pl.ds(i * PART, PART), :], keys[slab(k)].reshape(512, WIDE))

    def absorb(k, i, scores):
        rows = pl.ds(i * PART, PART)
        if k == 0:
            own = xh * 256 + c * ROWS
            token = lax.rem(lax.broadcasted_iota(jnp.int32, (PART, 512), 0), ROWS)
            later = lax.broadcasted_iota(jnp.int32, (PART, 512), 1) - own
            scores = jnp.where((later > token) & (later < ROWS), HIDDEN, scores)
        most = jnp.max(scores, axis=1, keepdims=True)
        if k != 0:
            before = top[rows, :1]
            most = jnp.maximum(most, before)
            fade = jnp.exp2((before - most) * factor)
        expo = jnp.exp2((scores - most) * factor)
        mass = (expo[:, :128] + expo[:, 128:256]) + (expo[:, 256:384] + expo[:, 384:])
        values = keys[slab(k), :, :, :, :KV_RANK].reshape(512, KV_RANK)
        gained = jnp.dot(expo.astype(BF16), values, preferred_element_type=F32)
        if k == 0:
            summed[rows, :] = gained
            total[rows, :] = mass
        else:
            summed[rows, :] = summed[rows, :] * fade + gained
            total[rows, :] = total[rows, :] * fade + mass
        top[rows, :] = jnp.broadcast_to(most, (PART, 128))

    def attend(k):
        count = HEADS * ROWS // PART
        following = scores_of(k, 0)
        for i in range(count):
            scores = following
            if i + 1 < count:
                following = scores_of(k, i + 1)
            absorb(k, i, scores)

    slots = {-1: 0, 1: 1, -2: 2, 2: 3, -3: 4, 3: 5, 4: 6}

    def pass_on(k):
        i, block = slots[k], slab(k)
        mine = keys.at[block, :, c, quarter(0)]
        push(mine, mine, n_send.at[0, i], n_recv.at[0, i], above)
        push(mine, mine, n_send.at[1, i], n_recv.at[1, i], below)
        first, second = keys.at[block, :, c, quarter(0, 0, 16)], keys.at[block, :, c, quarter(0, 16, 16)]
        push(first, first, n_send.at[2, i], n_recv.at[2, i], beside)
        push(second, second, n_send.at[3, i], n_recv.at[3, i], across)

    def from_z(d):
        for k, way, forward in ((-d, 0, right), (d, 1, left)):
            if d < 4:
                ref = keys.at[slab(k), :, c, quarter(0)]
                landed(ref, z_send.at[way, d - 1], z_recv.at[way, d - 1])
                if d == 3:
                    ref = keys.at[slab(k), way, c, quarter(0)]
                push(ref, ref, z_send.at[way, d], z_recv.at[way, d], forward)
                pass_on(k)
            else:
                ref = keys.at[slab(4), way, c, quarter(0)]
                landed(ref, z_send.at[way, 3], z_recv.at[way, 3])
        if d == 4:
            pass_on(4)

    def from_plane(k):
        i, block = slots[k], slab(k)
        landed(keys.at[block, :, c, quarter(3)], n_send.at[0, i], n_recv.at[0, i])
        landed(keys.at[block, :, c, quarter(1)], n_send.at[1, i], n_recv.at[1, i])
        landed(keys.at[block, :, c, quarter(2, 0, 16)], n_send.at[2, i], n_recv.at[2, i])
        landed(keys.at[block, :, c, quarter(2, 16, 16)], n_send.at[3, i], n_recv.at[3, i])
        whole = keys.at[block, :, c]
        push(whole, whole, d_send.at[i], d_recv.at[i], partner)

    def ready(k):
        landed(keys.at[slab(k), :, 1 - c], d_send.at[slots[k]], d_recv.at[slots[k]])

    rest = keys.at[z, 1 - xh, c, pl.ds(0, 96)]
    landed(rest, x_send.at[1], x_recv.at[1])
    push(keys.at[z, 1 - xh, c], keys.at[z, 1 - xh, c], c_send.at[1], c_recv.at[1], partner)
    w_copy = load(w_hbm, w_own, 6)
    push(w_hbm, w_own, w_send.at[1], w_recv.at[1], partner)
    landed(keys.at[z, xh, 1 - c], c_send.at[0], c_recv.at[0])
    landed(keys.at[z, 1 - xh, 1 - c], c_send.at[1], c_recv.at[1])
    attend(0)
    from_z(1)
    w_piece(0)
    w_piece(1)
    from_z(2)
    w_piece(2)
    from_plane(-1)
    from_plane(1)
    ready(-1)
    attend(-1)
    from_z(3)
    w_piece(3)
    ready(1)
    attend(1)
    from_plane(-2)
    from_plane(2)
    ready(-2)
    attend(-2)
    from_z(4)
    w_piece(4)
    w_piece(5)
    w_piece(6)
    ready(2)
    attend(2)
    from_plane(-3)
    from_plane(3)
    ready(-3)
    attend(-3)
    from_plane(4)
    ready(3)
    attend(3)
    ready(4)
    attend(4)

    for p in (0, 1):
        for h in range(4 * p, 4 * p + 4):
            rows = pl.ds(h * ROWS, ROWS)
            share = summed[rows, :] / jnp.sum(total[rows, :], axis=1, keepdims=True)
            value = jnp.dot(share.astype(BF16), up[:, h * 256 + NOPE : (h + 1) * 256], preferred_element_type=F32)
            held[z, p, :, (h - 4 * p) * VDIM : (h - 4 * p + 1) * VDIM] = value.astype(BF16)
        ref = held.at[z, p]
        push(ref, ref, a_send.at[0, 0, p], a_recv.at[0, 0, p], right)
        push(ref, ref, a_send.at[1, 0, p], a_recv.at[1, 0, p], left)
    w_other = w.at[pl.ds(pl.multiple_of(((1 - xh) * 2 + c) * 224, 32), 224)]
    landed(w_other, w_send.at[0], w_recv.at[0])
    push(w_other, w_other, w_send.at[2], w_recv.at[2], partner)
    w_copy.wait()
    landed(w_other, w_send.at[1], w_recv.at[1])
    landed(w_other, w_send.at[2], w_recv.at[2])
    mine = pl.ds(pl.multiple_of(head * 16, 16), 16)

    def multiply(k):
        block = slab(k)
        product = dot_nt(held[block, 0], w[:, :512]) + dot_nt(held[block, 1], w[:, 512:])
        part[block] = product.astype(BF16)
        for j in range(1, 8):
            rows = pl.ds(pl.multiple_of(lax.rem(head + j, 8) * 16, 16), 16)
            remote(
                part.at[block, rows], reached.at[block, j - 1], s_send.at[block], s_recv.at[block], seat(z, head + j)
            ).start()

    def collect(k):
        block = slab(k)
        landed(reached.at[block], s_send.at[block], s_recv.at[block])
        acc = part[block, mine].astype(F32)
        for j in range(7):
            acc = acc + reached[block, j].astype(F32)
        done[block] = acc.astype(BF16)
        if k == 0:

            @pl.when(head == z)
            def _():
                pltpu.make_async_copy(done.at[block], final.at[mine], f_recv).start()

            @pl.when(head != z)
            def _():
                remote(done.at[block], final.at[mine], f_send.at[0], f_recv, seat(block, z)).start()
        else:
            push(done.at[block], final.at[mine], f_send.at[k + 3], f_recv, seat(block, z))

    multiply(0)
    for d in (1, 2, 3):
        for p in (0, 1):
            for k, way, forward in ((-d, 0, right), (d, 1, left)):
                ref = held.at[slab(k), p]
                landed(ref, a_send.at[way, d - 1, p], a_recv.at[way, d - 1, p])
                if d < 3 or p == way:
                    push(ref, ref, a_send.at[way, d, p], a_recv.at[way, d, p], forward)
        multiply(-d)
        multiply(d)
        if d == 1:
            collect(0)
        else:
            collect(1 - d)
            collect(d - 1)
    for way in (0, 1):
        landed(held.at[slab(4), way], a_send.at[way, 3, way], a_recv.at[way, 3, way])
    multiply(4)
    collect(-3)
    collect(3)
    collect(4)
    landed(final, f_send.at[0], f_recv)
    out_ref[...] = final[...]
    for copy in sent:
        copy.wait_send()
    remote(rest, rest, x_send.at[1], x_recv.at[1], across).wait_send()
    remote(w_other, w_other, w_send.at[0], w_recv.at[0], opposite).wait_send()
    for block in range(8):
        remote(reached.at[block], reached.at[block], s_send.at[block], s_recv.at[block], right).wait_send()

    @pl.when(head != z)
    def _():
        remote(done.at[0], done.at[0], f_send.at[0], f_recv, right).wait_send()


def local(q_nope, q_rope, kv_latent, positions, kv_gain, kv_up, w_out):
    dma = pltpu.SemaphoreType.DMA
    columns, depth = 4 * w_out.shape[1], w_out.shape[0]
    any_ = pl.BlockSpec(memory_space=pl.ANY)
    return pl.pallas_call(
        kernel,
        out_shape=jax.ShapeDtypeStruct((ROWS, columns), BF16),
        in_specs=[any_] * 7,
        out_specs=pl.BlockSpec(memory_space=pltpu.VMEM),
        scratch_shapes=[
            pltpu.SMEM((ROWS,), jnp.int32),
            pltpu.VMEM((KV_RANK + ROPE, ROWS), BF16),
            pltpu.VMEM((KV_RANK,), F32),
            pltpu.VMEM((8, 2, 2, ROWS, WIDE), BF16),
            pltpu.VMEM((ROWS, HEADS * NOPE), BF16),
            pltpu.VMEM((ROWS, HEADS * ROPE), BF16),
            pltpu.VMEM((KV_RANK, HEADS * 256), BF16),
            pltpu.VMEM((HEADS * ROWS, WIDE), BF16),
            pltpu.VMEM((HEADS * ROWS, 128), F32),
            pltpu.VMEM((HEADS * ROWS, 128), F32),
            pltpu.VMEM((HEADS * ROWS, KV_RANK), F32),
            pltpu.VMEM((8, 2, ROWS, depth // 2), BF16),
            pltpu.VMEM((columns, depth), BF16),
            pltpu.VMEM((8, ROWS, columns), BF16),
            pltpu.VMEM((8, 7, 16, columns), BF16),
            pltpu.VMEM((8, 16, columns), BF16),
            pltpu.VMEM((ROWS, columns), BF16),
            dma((7,)), dma((2,)), dma((2,)), dma((2,)), dma((2,)), dma((2, 4)), dma((2, 4)),
            dma((4, 7)), dma((4, 7)), dma((7,)), dma((7,)),
            dma((3,)), dma((3,)), dma((2, 4, 2)), dma((2, 4, 2)), dma((8,)), dma((8,)), dma((8,)), dma(()),
        ],
        compiler_params=pltpu.CompilerParams(
            collective_id=0, has_side_effects=True, vmem_limit_bytes=60 * 2**20
        ),
        cost_estimate=pl.CostEstimate(flops=13 * 10**9, bytes_accessed=4 * 10**6, transcendentals=4 * 10**6),
        name="attention",
    )(positions, kv_latent.T, kv_gain, q_nope, q_rope, kv_up, w_out.T)


def solution(mesh):
    return jax.shard_map(
        local,
        mesh=mesh,
        in_specs=(
            P("seq", "head"),
            P("seq", "head"),
            P("seq", None),
            P("seq"),
            P(),
            P(None, "head"),
            P("head", "seq"),
        ),
        out_specs=P("seq", "head"),
        check_vma=False,
    )
```

time: 474 us -> 89.1 us (0.19)
  waiting for transfers between devices: 264 us -> 0 us
  Pallas kernels: 0 us -> 87.4 us
  matrix products: 60 us -> 0 us
  local copies, waits for them, and re-layouts: 56.4 us -> 1.65 us
  blocking collectives: 43.7 us -> 0 us
  other arithmetic: 30.3 us -> 0 us
  between operations: 13.6 us -> 0.01 us
    ppermute x31 -> x0, waiting for transfers between devices: 222 us -> none  [shifted(): return lax.ppermute(block, axis, route)]
    pallas_call x0 -> x1, Pallas kernels: none -> 87.4 us  [local(): pl.pallas_call(kernel, out_shape=jax.ShapeDtypeStruct((ROWS, columns), BF...]
    dot_general x129 -> x0, matrix products: 60 us -> none  [the longest x32 16.7 us: update(): jnp.dot(block[:, :KV_RANK], kv_up, preferred_element_type=jnp.float32)]
    all_gather x1 -> x0, blocking collectives: 43.7 us -> none  [local(): all_positions = lax.all_gather(positions, 'seq', axis=0, tiled=True)]
    unnamed x3 -> x0, waiting for transfers between devices: 41.9 us -> none
    while x95 -> x0, local copies, waits for them, and re-layouts: 24.4 us -> none
    ge x32 -> x0, other arithmetic: 23.6 us -> none  [update(): visible = positions[:, None] >= key_pos[None, :]]
    dynamic_slice x32 -> x0, local copies, waits for them, and re-layouts: 23.3 us -> none  [attend(): key_pos = lax.dynamic_slice_in_dim(all_positions, anchor * width, width)]
  transfers between devices with their start and end apart: 33 -> 0, of which waited for: 32 -> 0; matrix products, arithmetic and copies ran while one was open for 28% -> 0% of each run, Pallas kernels for 0% -> 0%
where the time goes in v3:
time: 89.1 us; the launch traced here: 89 us
  Pallas kernels  87.4 us (98%)
  local copies, waits for them, and re-layouts  1.65 us (2%)
    pallas_call x1, Pallas kernels, local(): pl.pallas_call(kernel, out_shape=jax.ShapeDtypeStruct((ROWS, columns), BF...  87.4 us

profile of v3, /device:TPU:2, one launch (start us, length us, event | category | flops | bytes accessed | tf_op | source)
XLA Modules:
  0.0 89.0 jit_solution(9638020279638669726)
XLA Ops:
  0.0 87.4 %attention.1 = bf16[128,896]{1,0:T(8,128)(2,1)} custom-call(s32[128]{0:T(128)} %pos_hbm.1, bf16[576,128]{1,0:T(8,128)(2,1)} %bitcast.3, f32[512]{0:T(512)} %gain_hbm.1, bf16[128,1024]{1,0:T(8,128)(2,1)} %qn_hbm.1, bf16[128,512]{1,0:T(8,128)(2,1)} %qr_hbm.1, bf16[512,2048]{1,0:T(8,128)(2,1)} %up_hbm.1, bf16[224,1024]{1,0:T(8,128)(2,1)} %bitcast.2), custom_call_target="tpu_custom_call" | custom-call | flops 12999999488 | bytes 4000000 | tf_op jit(solution)/shard_map/attention/pallas_call | solution.py:332
  87.4 1.6 %copy.9 = bf16[128,896]{1,0:T(8,128)(2,1)} copy(bf16[128,896]{1,0:T(8,128)(2,1)} %attention.1) | data formatting | bytes 458752

commit v4 on v3

--- a/solution.py
+++ b/solution.py
@@ -78,7 +78,7 @@
     def greet(peer):
         pl.semaphore_signal(barrier, inc=1, device_id=peer, device_id_type=MESH)
 
-    for peer in (across, partner, opposite, right, left):
+    for peer in (across, partner, opposite, right, left, at(z + 1, 1 - xh, c, 1 - xl, y), at(z - 1, 1 - xh, c, 1 - xl, y)):
         greet(peer)
     for j in range(1, 8):
         greet(seat(z, head + j))
@@ -95,35 +95,35 @@
     rope = lat_ref[KV_RANK:, :].astype(F32)
     tail = jnp.concatenate([rope, jnp.zeros((64, ROWS), F32)], axis=0).T
     keys[z, xh, c, :, KV_RANK:] = jnp.where(lane == 64 + block_no, 1.0, tail).astype(BF16)
-    pl.semaphore_wait(barrier, jnp.where(head == z, 19, 20))
+    pl.semaphore_wait(barrier, jnp.where(head == z, 21, 22))
 
     colour = lax.rem(2 * (2 * xh + xl) + y, 4)
 
     def quarter(i, start=0, size=32):
         return pl.ds(pl.multiple_of(lax.rem(colour + i, 4) * 32 + start, 16), size)
 
-    push(keys.at[z, xh, c, quarter(2)], keys.at[z, xh, c, quarter(2)], x_send.at[0], x_recv.at[0], across)
+    first, second = keys.at[z, xh, c, quarter(0)], keys.at[z, xh, c, quarter(2)]
+    for way, step in ((0, 1), (1, -1)):
+        push(first, first, z_send.at[way, 0, 0], z_recv.at[way, 0, 0], at(z + step, xh, c, xl, y))
+        push(second, second, z_send.at[way, 0, 1], z_recv.at[way, 0, 1], at(z + step, 1 - xh, c, 1 - xl, y))
+    push(keys.at[z, xh, c], keys.at[z, xh, c], x_send.at[0], x_recv.at[0], across)
     push(keys.at[z, xh, c], keys.at[z, xh, c], c_send.at[0], c_recv.at[0], partner)
-    for i in (0, 1, 3):
-        ref = keys.at[z, xh, c, quarter(i)]
-        remote(ref, ref, x_send.at[1], x_recv.at[1], across).start()
 
     factor = math.log2(math.e) / math.sqrt(NOPE + ROPE)
     for copy in loads:
         copy.wait()
     ahead = jnp.where((lane >= 64) & (lane - 64 > block_no) & (lane < 96), HIDDEN, 0.0)
-    for h in range(HEADS):
+
+    def fold(h):
         rows = pl.ds(h * ROWS, ROWS)
         folded = dot_nt(qn[:, h * NOPE : (h + 1) * NOPE], up[:, h * 256 : h * 256 + NOPE])
         query[rows, :KV_RANK] = folded.astype(BF16)
         turned = qr[:, h * ROPE : (h + 1) * ROPE].astype(F32)
         turned = jnp.concatenate([turned, jnp.zeros((ROWS, 64), F32)], axis=1)
         query[rows, KV_RANK:] = (turned + ahead).astype(BF16)
-        if h == 1:
-            landed(keys.at[z, 1 - xh, c, quarter(0)], x_send.at[0], x_recv.at[0])
-            start = keys.at[z, :, c, quarter(0)]
-            push(start, start, z_send.at[0, 0], z_recv.at[0, 0], right)
-            push(start, start, z_send.at[1, 0], z_recv.at[1, 0], left)
+
+    for h in range(4):
+        fold(h)
 
     def w_piece(i):
         piece = pl.ds(pl.multiple_of((xh * 2 + c) * 224 + i * 32, 32), 32)
@@ -156,7 +156,7 @@
             total[rows, :] = total[rows, :] * fade + mass
         top[rows, :] = jnp.broadcast_to(most, (PART, 128))
 
-    def attend(k):
+    def attend(k, finish=None):
         count = HEADS * ROWS // PART
         following = scores_of(k, 0)
         for i in range(count):
@@ -164,6 +164,8 @@
             if i + 1 < count:
                 following = scores_of(k, i + 1)
             absorb(k, i, scores)
+            if finish is not None and (i + 1) % (count // 2) == 0:
+                finish((i + 1) // (count // 2) - 1)
 
     slots = {-1: 0, 1: 1, -2: 2, 2: 3, -3: 4, 3: 5, 4: 6}
 
@@ -177,19 +179,16 @@
         push(second, second, n_send.at[3, i], n_recv.at[3, i], across)
 
     def from_z(d):
-        for k, way, forward in ((-d, 0, right), (d, 1, left)):
-            if d < 4:
-                ref = keys.at[slab(k), :, c, quarter(0)]
-                landed(ref, z_send.at[way, d - 1], z_recv.at[way, d - 1])
-                if d == 3:
-                    ref = keys.at[slab(k), way, c, quarter(0)]
-                push(ref, ref, z_send.at[way, d], z_recv.at[way, d], forward)
-                pass_on(k)
-            else:
-                ref = keys.at[slab(4), way, c, quarter(0)]
-                landed(ref, z_send.at[way, 3], z_recv.at[way, 3])
-        if d == 4:
-            pass_on(4)
+        for t in (0, 1):
+            kind = xh if t == 0 else 1 - xh
+            for k, way, forward in ((-d, 0, right), (d, 1, left)):
+                ref = keys.at[slab(k), kind, c, quarter(0)]
+                if d < 4 or t == way:
+                    landed(ref, z_send.at[way, d - 1, t], z_recv.at[way, d - 1, t])
+                if d < 3 or (d == 3 and t == way):
+                    push(ref, ref, z_send.at[way, d, t], z_recv.at[way, d, t], forward)
+        for k in (-d, d) if d < 4 else (4,):
+            pass_on(k)
 
     def from_plane(k):
         i, block = slots[k], slab(k)
@@ -203,48 +202,49 @@
     def ready(k):
         landed(keys.at[slab(k), :, 1 - c], d_send.at[slots[k]], d_recv.at[slots[k]])
 
-    rest = keys.at[z, 1 - xh, c, pl.ds(0, 96)]
-    landed(rest, x_send.at[1], x_recv.at[1])
-    push(keys.at[z, 1 - xh, c], keys.at[z, 1 - xh, c], c_send.at[1], c_recv.at[1], partner)
+    from_z(1)
+    for h in range(4, 8):
+        fold(h)
+    from_z(2)
+    theirs = keys.at[z, 1 - xh, c]
+    landed(theirs, x_send.at[0], x_recv.at[0])
+    push(theirs, theirs, c_send.at[1], c_recv.at[1], partner)
     w_copy = load(w_hbm, w_own, 6)
-    push(w_hbm, w_own, w_send.at[1], w_recv.at[1], partner)
+    w_piece(0)
+    from_z(3)
+    from_plane(-1)
+    from_plane(1)
     landed(keys.at[z, xh, 1 - c], c_send.at[0], c_recv.at[0])
     landed(keys.at[z, 1 - xh, 1 - c], c_send.at[1], c_recv.at[1])
     attend(0)
-    from_z(1)
-    w_piece(0)
+    from_z(4)
     w_piece(1)
-    from_z(2)
     w_piece(2)
-    from_plane(-1)
-    from_plane(1)
+    w_piece(3)
+    from_plane(-2)
     ready(-1)
     attend(-1)
-    from_z(3)
-    w_piece(3)
-    ready(1)
-    attend(1)
-    from_plane(-2)
     from_plane(2)
-    ready(-2)
-    attend(-2)
-    from_z(4)
     w_piece(4)
     w_piece(5)
     w_piece(6)
+    push(w_hbm, w_own, w_send.at[1], w_recv.at[1], partner)
+    ready(1)
+    attend(1)
+    from_plane(-3)
+    ready(-2)
+    attend(-2)
+    from_plane(3)
     ready(2)
     attend(2)
-    from_plane(-3)
-    from_plane(3)
+    from_plane(4)
     ready(-3)
     attend(-3)
-    from_plane(4)
     ready(3)
     attend(3)
     ready(4)
-    attend(4)
-
-    for p in (0, 1):
+
+    def finish(p):
         for h in range(4 * p, 4 * p + 4):
             rows = pl.ds(h * ROWS, ROWS)
             share = summed[rows, :] / jnp.sum(total[rows, :], axis=1, keepdims=True)
@@ -253,6 +253,16 @@
         ref = held.at[z, p]
         push(ref, ref, a_send.at[0, 0, p], a_recv.at[0, 0, p], right)
         push(ref, ref, a_send.at[1, 0, p], a_recv.at[1, 0, p], left)
+
+    attend(4, finish)
+
+    earlier = sent[:-4]
+    del sent[:-4]
+
+    def flush(copies):
+        for copy in copies:
+            copy.wait_send()
+
     w_other = w.at[pl.ds(pl.multiple_of(((1 - xh) * 2 + c) * 224, 32), 224)]
     landed(w_other, w_send.at[0], w_recv.at[0])
     push(w_other, w_other, w_send.at[2], w_recv.at[2], partner)
@@ -290,39 +300,53 @@
         else:
             push(done.at[block], final.at[mine], f_send.at[k + 3], f_recv, seat(block, z))
 
+    def from_ring(d, p):
+        for k, way, forward in ((-d, 0, right), (d, 1, left)):
+            ref = held.at[slab(k), p]
+            landed(ref, a_send.at[way, d - 1, p], a_recv.at[way, d - 1, p])
+            if d < 3 or p == way:
+                push(ref, ref, a_send.at[way, d, p], a_recv.at[way, d, p], forward)
+
     multiply(0)
-    for d in (1, 2, 3):
-        for p in (0, 1):
-            for k, way, forward in ((-d, 0, right), (d, 1, left)):
-                ref = held.at[slab(k), p]
-                landed(ref, a_send.at[way, d - 1, p], a_recv.at[way, d - 1, p])
-                if d < 3 or p == way:
-                    push(ref, ref, a_send.at[way, d, p], a_recv.at[way, d, p], forward)
-        multiply(-d)
-        multiply(d)
-        if d == 1:
-            collect(0)
-        else:
-            collect(1 - d)
-            collect(d - 1)
+    flush(earlier)
+    remote(w_other, w_other, w_send.at[0], w_recv.at[0], opposite).wait_send()
+    from_ring(1, 0)
+    from_ring(1, 1)
+    multiply(-1)
+    multiply(1)
+    from_ring(2, 0)
+    collect(0)
+    from_ring(2, 1)
+    multiply(-2)
+    multiply(2)
+    from_ring(3, 0)
+    collect(-1)
+    collect(1)
+    from_ring(3, 1)
+    multiply(-3)
+    multiply(3)
+    collect(-2)
+    collect(2)
     for way in (0, 1):
         landed(held.at[slab(4), way], a_send.at[way, 3, way], a_recv.at[way, 3, way])
     multiply(4)
+    flush(sent)
+    sent.clear()
+    for k in (0, -1, 1, -2, 2):
+        remote(reached.at[slab(k)], reached.at[slab(k)], s_send.at[slab(k)], s_recv.at[slab(k)], right).wait_send()
     collect(-3)
     collect(3)
     collect(4)
-    landed(final, f_send.at[0], f_recv)
-    out_ref[...] = final[...]
-    for copy in sent:
-        copy.wait_send()
-    remote(rest, rest, x_send.at[1], x_recv.at[1], across).wait_send()
-    remote(w_other, w_other, w_send.at[0], w_recv.at[0], opposite).wait_send()
-    for block in range(8):
-        remote(reached.at[block], reached.at[block], s_send.at[block], s_recv.at[block], right).wait_send()
+    for k in (-3, 3, 4):
+        remote(reached.at[slab(k)], reached.at[slab(k)], s_send.at[slab(k)], s_recv.at[slab(k)], right).wait_send()
+    flush(sent)
 
     @pl.when(head != z)
     def _():
         remote(done.at[0], done.at[0], f_send.at[0], f_recv, right).wait_send()
+
+    landed(final, f_send.at[0], f_recv)
+    out_ref[...] = final[...]
 
 
 def local(q_nope, q_rope, kv_latent, positions, kv_gain, kv_up, w_out):
@@ -352,9 +376,10 @@
             pltpu.VMEM((8, 7, 16, columns), BF16),
             pltpu.VMEM((8, 16, columns), BF16),
             pltpu.VMEM((ROWS, columns), BF16),
-            dma((7,)), dma((2,)), dma((2,)), dma((2,)), dma((2,)), dma((2, 4)), dma((2, 4)),
+            dma((7,)), dma((1,)), dma((1,)), dma((2,)), dma((2,)), dma((2, 4, 2)), dma((2, 4, 2)),
             dma((4, 7)), dma((4, 7)), dma((7,)), dma((7,)),
-            dma((3,)), dma((3,)), dma((2, 4, 2)), dma((2, 4, 2)), dma((8,)), dma((8,)), dma((8,)), dma(()),
+            dma((3,)), dma((3,)), dma((2, 4, 2)), dma((2, 4, 2)),
+            dma((8,)), dma((8,)), dma((8,)), dma(()),
         ],
         compiler_params=pltpu.CompilerParams(
             collective_id=0, has_side_effects=True, vmem_limit_bytes=60 * 2**20

time: 89.1 us -> 81.3 us (0.912)
  Pallas kernels: 87.4 us -> 79.5 us
    pallas_call x1, Pallas kernels: 87.4 us -> 79.5 us  [local(): pl.pallas_call(kernel, out_shape=jax.ShapeDtypeStruct((ROWS, columns), BF...]
where the time goes in v4:
time: 81.3 us; the launch traced here: 81.1 us
  Pallas kernels  79.5 us (98%)
  local copies, waits for them, and re-layouts  1.65 us (2%)
    pallas_call x1, Pallas kernels, local(): pl.pallas_call(kernel, out_shape=jax.ShapeDtypeStruct((ROWS, columns), BF...  79.5 us
    unnamed x1, local copies, waits for them, and re-layouts  1.65 us

profile of v4, /device:TPU:2, one launch (start us, length us, event | category | flops | bytes accessed | tf_op | source)
XLA Modules:
  0.0 81.1 jit_solution(6561497657663498906)
XLA Ops:
  0.0 79.5 %attention.1 = bf16[128,896]{1,0:T(8,128)(2,1)} custom-call(s32[128]{0:T(128)} %pos_hbm.1, bf16[576,128]{1,0:T(8,128)(2,1)} %bitcast.3, f32[512]{0:T(512)} %gain_hbm.1, bf16[128,1024]{1,0:T(8,128)(2,1)} %qn_hbm.1, bf16[128,512]{1,0:T(8,128)(2,1)} %qr_hbm.1, bf16[512,2048]{1,0:T(8,128)(2,1)} %up_hbm.1, bf16[224,1024]{1,0:T(8,128)(2,1)} %bitcast.2), custom_call_target="tpu_custom_call" | custom-call | flops 12999999488 | bytes 4000000 | tf_op jit(solution)/shard_map/attention/pallas_call | solution.py:356
  79.5 1.6 %copy.9 = bf16[128,896]{1,0:T(8,128)(2,1)} copy(bf16[128,896]{1,0:T(8,128)(2,1)} %attention.1) | data formatting | bytes 458752

commit v5 on v4

--- a/solution.py
+++ b/solution.py
@@ -28,9 +28,9 @@
 def kernel(
     pos_hbm, lat_hbm, gain_hbm, qn_hbm, qr_hbm, up_hbm, w_hbm, out_ref,
     pos_ref, lat_ref, gain_ref, keys, qn, qr, up, query, top, total, summed,
-    held, w, part, reached, done, final,
+    held, w, part, half, strips, sums, reached, done, final,
     local_sem, x_send, x_recv, c_send, c_recv, z_send, z_recv, n_send, n_recv, d_send, d_recv,
-    w_send, w_recv, a_send, a_recv, s_send, s_recv, f_send, f_recv,
+    w_send, w_recv, a_send, a_recv, p_send, p_recv, s_send, s_recv, f_send, f_recv,
 ):
     s, head = lax.axis_index("seq"), lax.axis_index("head")
     z, xh, c, xl, y = s // 4, lax.rem(s // 2, 2), lax.rem(s, 2), head // 4, lax.rem(head, 4)
@@ -271,21 +271,59 @@
     landed(w_other, w_send.at[2], w_recv.at[2])
     mine = pl.ds(pl.multiple_of(head * 16, 16), 16)
 
+    lot = pl.ds(pl.multiple_of(y * 16, 16), 16)
+
+    def lot_of(j):
+        return pl.ds(pl.multiple_of(lax.rem(y + j, 4) * 16, 16), 16)
+
     def multiply(k):
         block = slab(k)
         product = dot_nt(held[block, 0], w[:, :512]) + dot_nt(held[block, 1], w[:, 512:])
-        part[block] = product.astype(BF16)
-        for j in range(1, 8):
-            rows = pl.ds(pl.multiple_of(lax.rem(head + j, 8) * 16, 16), 16)
-            remote(
-                part.at[block, rows], reached.at[block, j - 1], s_send.at[block], s_recv.at[block], seat(z, head + j)
-            ).start()
+        part[block] = product.astype(BF16).reshape(2, 64, product.shape[1])
+        if k == -3:
+            push(part.at[block, 1 - xl], half, p_send.at[0], p_recv.at[0], beside)
+        elif k == 3:
+            for j in (1, 2, 3):
+                remote(
+                    part.at[block, :, lot_of(j)], strips.at[j - 1], p_send.at[1], p_recv.at[1], at(z, xh, c, xl, y + j)
+                ).start()
+        else:
+            for j in range(1, 8):
+                t = lax.rem(head + j, 8)
+                rows = pl.ds(pl.multiple_of(lax.rem(t, 4) * 16, 16), 16)
+                remote(
+                    part.at[block, t // 4, rows], reached.at[block, j - 1], s_send.at[block], s_recv.at[block], seat(z, t)
+                ).start()
+
+    def relay(k):
+        block = slab(k)
+        if k == -3:
+            landed(half, p_send.at[0], p_recv.at[0])
+            half[...] = (part[block, xl].astype(F32) + half[...].astype(F32)).astype(BF16)
+            for j in (1, 2, 3):
+                remote(
+                    half.at[lot_of(j)], reached.at[block, j - 1], s_send.at[block], s_recv.at[block],
+                    at(z, xh, c, xl, y + j),
+                ).start()
+        else:
+            landed(strips, p_send.at[1], p_recv.at[1])
+            acc = part[block, :, lot].astype(F32)
+            for j in range(3):
+                acc = acc + strips[j].astype(F32)
+            sums[...] = acc.astype(BF16)
+            push(sums.at[1 - xl], reached.at[block, 0], s_send.at[block], s_recv.at[block], beside)
 
     def collect(k):
         block = slab(k)
-        landed(reached.at[block], s_send.at[block], s_recv.at[block])
-        acc = part[block, mine].astype(F32)
-        for j in range(7):
+        pieces = {-3: 3, 3: 1}.get(k, 7)
+        landed(reached.at[block, pl.ds(0, pieces)], s_send.at[block], s_recv.at[block])
+        if k == -3:
+            acc = half[lot].astype(F32)
+        elif k == 3:
+            acc = sums[xl].astype(F32)
+        else:
+            acc = part[block, xl, lot].astype(F32)
+        for j in range(pieces):
             acc = acc + reached[block, j].astype(F32)
         done[block] = acc.astype(BF16)
         if k == 0:
@@ -330,14 +368,17 @@
     for way in (0, 1):
         landed(held.at[slab(4), way], a_send.at[way, 3, way], a_recv.at[way, 3, way])
     multiply(4)
-    flush(sent)
-    sent.clear()
+    relay(-3)
+    relay(3)
+    collect(4)
+    collect(-3)
+    collect(3)
     for k in (0, -1, 1, -2, 2):
         remote(reached.at[slab(k)], reached.at[slab(k)], s_send.at[slab(k)], s_recv.at[slab(k)], right).wait_send()
-    collect(-3)
-    collect(3)
-    collect(4)
-    for k in (-3, 3, 4):
+    pieces = reached.at[slab(-3), pl.ds(0, 3)]
+    remote(pieces, pieces, s_send.at[slab(-3)], s_recv.at[slab(-3)], right).wait_send()
+    remote(strips, strips, p_send.at[1], p_recv.at[1], right).wait_send()
+    for k in (4,):
         remote(reached.at[slab(k)], reached.at[slab(k)], s_send.at[slab(k)], s_recv.at[slab(k)], right).wait_send()
     flush(sent)
 
@@ -355,7 +396,7 @@
     any_ = pl.BlockSpec(memory_space=pl.ANY)
     return pl.pallas_call(
         kernel,
-        out_shape=jax.ShapeDtypeStruct((ROWS, columns), BF16),
+        out_shape=pltpu.VMEM((ROWS, columns), BF16),
         in_specs=[any_] * 7,
         out_specs=pl.BlockSpec(memory_space=pltpu.VMEM),
         scratch_shapes=[
@@ -372,14 +413,17 @@
             pltpu.VMEM((HEADS * ROWS, KV_RANK), F32),
             pltpu.VMEM((8, 2, ROWS, depth // 2), BF16),
             pltpu.VMEM((columns, depth), BF16),
-            pltpu.VMEM((8, ROWS, columns), BF16),
+            pltpu.VMEM((8, 2, 64, columns), BF16),
+            pltpu.VMEM((64, columns), BF16),
+            pltpu.VMEM((3, 2, 16, columns), BF16),
+            pltpu.VMEM((2, 16, columns), BF16),
             pltpu.VMEM((8, 7, 16, columns), BF16),
             pltpu.VMEM((8, 16, columns), BF16),
             pltpu.VMEM((ROWS, columns), BF16),
             dma((7,)), dma((1,)), dma((1,)), dma((2,)), dma((2,)), dma((2, 4, 2)), dma((2, 4, 2)),
             dma((4, 7)), dma((4, 7)), dma((7,)), dma((7,)),
             dma((3,)), dma((3,)), dma((2, 4, 2)), dma((2, 4, 2)),
-            dma((8,)), dma((8,)), dma((8,)), dma(()),
+            dma((2,)), dma((2,)), dma((8,)), dma((8,)), dma((8,)), dma(()),
         ],
         compiler_params=pltpu.CompilerParams(
             collective_id=0, has_side_effects=True, vmem_limit_bytes=60 * 2**20

time: 81.3 us -> 78.8 us (0.969)
  Pallas kernels: 79.5 us -> 78 us
  local copies, waits for them, and re-layouts: 1.65 us -> 0.69 us
    pallas_call x1, Pallas kernels: 79.5 us -> 78 us  [local(): pl.pallas_call(kernel, out_shape=pltpu.VMEM((ROWS, columns), BF16), in_sp...]
    unnamed x1, local copies, waits for them, and re-layouts: 1.65 us -> 0.69 us
where the time goes in v5:
time: 78.8 us; the launch traced here: 78.7 us
  Pallas kernels  78 us (99%)
    pallas_call x1, Pallas kernels, local(): pl.pallas_call(kernel, out_shape=pltpu.VMEM((ROWS, columns), BF16), in_sp...  78 us

profile of v5, /device:TPU:2, one launch (start us, length us, event | category | flops | bytes accessed | tf_op | source)
XLA Modules:
  0.0 78.7 jit_solution(173798836484065682)
XLA Ops:
  0.0 78.0 %attention.1 = bf16[128,896]{1,0:T(8,128)(2,1)S(1)} custom-call(s32[128]{0:T(128)} %pos_hbm.1, bf16[576,128]{1,0:T(8,128)(2,1)} %bitcast.3, f32[512]{0:T(512)} %gain_hbm.1, bf16[128,1024]{1,0:T(8,128)(2,1)} %qn_hbm.1, bf16[128,512]{1,0:T(8,128)(2,1)} %qr_hbm.1, bf16[512,2048]{1,0:T(8,128)(2,1)} %up_hbm.1, bf16[224,1024]{1,0:T(8,128)(2,1)} %bitcast.2), custom_call_target="tpu_custom_call" | custom-call | flops 12999999488 | bytes 4000000 | tf_op jit(solution)/shard_map/attention/pallas_call | solution.py:397
  78.0 0.7 copy.9

commit v6 on v5

--- a/solution.py
+++ b/solution.py
@@ -276,10 +276,15 @@
     def lot_of(j):
         return pl.ds(pl.multiple_of(lax.rem(y + j, 4) * 16, 16), 16)
 
-    def multiply(k):
+    def product(*offsets):
+        sides = [jnp.concatenate([held[slab(k), p] for k in offsets], axis=0) for p in (0, 1)]
+        both = dot_nt(sides[0], w[:, :512]) + dot_nt(sides[1], w[:, 512:])
+        for n, k in enumerate(offsets):
+            part[slab(k)] = both[n * ROWS : (n + 1) * ROWS].astype(BF16).reshape(2, 64, both.shape[1])
+            spread(k)
+
+    def spread(k):
         block = slab(k)
-        product = dot_nt(held[block, 0], w[:, :512]) + dot_nt(held[block, 1], w[:, 512:])
-        part[block] = product.astype(BF16).reshape(2, 64, product.shape[1])
         if k == -3:
             push(part.at[block, 1 - xl], half, p_send.at[0], p_recv.at[0], beside)
         elif k == 3:
@@ -345,29 +350,26 @@
             if d < 3 or p == way:
                 push(ref, ref, a_send.at[way, d, p], a_recv.at[way, d, p], forward)
 
-    multiply(0)
+    product(0)
     flush(earlier)
     remote(w_other, w_other, w_send.at[0], w_recv.at[0], opposite).wait_send()
     from_ring(1, 0)
     from_ring(1, 1)
-    multiply(-1)
-    multiply(1)
+    product(-1, 1)
     from_ring(2, 0)
     collect(0)
     from_ring(2, 1)
-    multiply(-2)
-    multiply(2)
+    product(-2, 2)
     from_ring(3, 0)
     collect(-1)
     collect(1)
     from_ring(3, 1)
-    multiply(-3)
-    multiply(3)
+    product(-3, 3)
     collect(-2)
     collect(2)
     for way in (0, 1):
         landed(held.at[slab(4), way], a_send.at[way, 3, way], a_recv.at[way, 3, way])
-    multiply(4)
+    product(4)
     relay(-3)
     relay(3)
     collect(4)

time: 78.8 us -> 78.6 us (level)
  no operation moved by 1% of the time
where the time goes in v6:
time: 78.6 us; the launch traced here: 78.1 us
  Pallas kernels  77.4 us (98%)
    pallas_call x1, Pallas kernels, local(): pl.pallas_call(kernel, out_shape=pltpu.VMEM((ROWS, columns), BF16), in_sp...  77.4 us

profile of v6, /device:TPU:2, one launch (start us, length us, event | category | flops | bytes accessed | tf_op | source)
XLA Modules:
  0.0 78.1 jit_solution(1427236055326377770)
XLA Ops:
  0.0 77.4 %attention.1 = bf16[128,896]{1,0:T(8,128)(2,1)S(1)} custom-call(s32[128]{0:T(128)} %pos_hbm.1, bf16[576,128]{1,0:T(8,128)(2,1)} %bitcast.3, f32[512]{0:T(512)} %gain_hbm.1, bf16[128,1024]{1,0:T(8,128)(2,1)} %qn_hbm.1, bf16[128,512]{1,0:T(8,128)(2,1)} %qr_hbm.1, bf16[512,2048]{1,0:T(8,128)(2,1)} %up_hbm.1, bf16[224,1024]{1,0:T(8,128)(2,1)} %bitcast.2), custom_call_target="tpu_custom_call" | custom-call | flops 12999999488 | bytes 4000000 | tf_op jit(solution)/shard_map/attention/pallas_call | solution.py:399
  77.4 0.7 copy.9
